TPU v7x, 32 devices: a whole 2x2x4 slice. The times are simulated.
32 devices in a mesh: gx: 4 (over y, x), gy: 8 (over z, core).
Axes of the slice: x: 2, y: 2, z: 4, core: 2. Of those that a mesh axis runs over, the one named last changes fastest.
Arguments:
- right_side: float32 [28, 56, 168], P('gx', 'gy'), may hold values from -18 to 18
- stiff_coef: float32 [4, 8, 24], P('gx', 'gy'), may hold values from 0.3 to 3
- mass_coef: float32 [4, 8, 24], P('gx', 'gy'), may hold values from 2 to 200
- coarse_factor: float32 [256, 256], P(('gx', 'gy')), may hold values from -0.0390625 to 0.0390625
Outputs:
- solution: float32 [28, 56, 168], P('gx', 'gy')
- residual: float32 [28, 56, 168], P('gx', 'gy')
All inputs are finite; a program needn't handle non-finite values.
Results may differ from a plain program's by a relative error of at most 0.0003.
Values sent between devices are 32-bit elements; how exact they have to be, the bound alone decides.
A program may use at most 64 MiB of HBM per device.

v0:
```python
import math

import jax
import jax.numpy as jnp
import numpy as np
from jax import lax
from jax.sharding import PartitionSpec as P

ITERS = 2


exact_mode = lax.Precision.HIGHEST


def with_halo(block, sides, width):
    for axis, dim in sides:
        count = lax.axis_size(axis)
        forward = [(i, i + 1) for i in range(count - 1)]
        forward.append((count - 1, 0))
        backward = [(target, source) for source, target in forward]
        low = lax.ppermute(
            lax.slice_in_dim(block, block.shape[dim] - width, None, axis=dim), axis, forward
        )
        high = lax.ppermute(lax.slice_in_dim(block, 0, width, axis=dim), axis, backward)
        block = jnp.concatenate([low, block, high], axis=dim)
    return block


def swapped(shard, axis, apart):
    return lax.ppermute(shard, axis, [(i, i ^ 1 << apart) for i in range(lax.axis_size(axis))])


def legendre_pair(position, degree):
    p_prev = 1.0
    p_now = position
    for order in range(2, degree + 1):
        p_next = ((2 * order - 1) * position * p_now - (order - 1) * p_prev) / order
        p_prev = p_now
        p_now = p_next
    return (p_now, p_prev)


def jacobi_eigen(matrix):
    size_n = matrix.shape[0]
    current = np.array(matrix)
    vectors = np.eye(size_n)
    for sweep in range(20):
        for row_p in range(size_n - 1):
            for row_q in range(row_p + 1, size_n):
                off_value = current[row_p, row_q]
                if abs(off_value) > 1e-300:
                    theta = (current[row_q, row_q] - current[row_p, row_p]) / (2.0 * off_value)
                    sign_t = 1.0 if theta >= 0.0 else -1.0
                    tangent = sign_t / (abs(theta) + math.sqrt(theta * theta + 1.0))
                    cosine = 1.0 / math.sqrt(tangent * tangent + 1.0)
                    sine = tangent * cosine
                    rotation = np.eye(size_n)
                    rotation[row_p, row_p] = cosine
                    rotation[row_q, row_q] = cosine
                    rotation[row_p, row_q] = sine
                    rotation[row_q, row_p] = -sine
                    current = rotation.T @ current @ rotation
                    vectors = vectors @ rotation
    return (np.array([current[idx, idx] for idx in range(size_n)]), vectors)


def gll_tables():
    degree = 7
    guesses = [
        -0.8717401485096066,
        -0.5917001814331423,
        -0.2092992179024789,
        0.2092992179024789,
        0.5917001814331423,
        0.8717401485096066,
    ]
    interior = []
    for guess in guesses:
        position = guess
        for newton in range(30):
            p_now, p_prev = legendre_pair(position, degree)
            first = degree * (position * p_now - p_prev) / (position * position - 1.0)
            second = (2.0 * position * first - degree * (degree + 1) * p_now) / (
                1.0 - position * position
            )
            position = position - first / second
        interior.append(position)
    points = np.array([-1.0] + interior + [1.0])
    values = np.array([legendre_pair(float(pt), degree)[0] for pt in points])
    weights = 2.0 / (degree * (degree + 1) * values**2)
    deriv_mat = np.zeros((8, 8))
    for left_idx in range(8):
        for right_idx in range(8):
            if left_idx != right_idx:
                deriv_mat[left_idx, right_idx] = values[left_idx] / (
                    values[right_idx] * (points[left_idx] - points[right_idx])
                )
    deriv_mat[0, 0] = -degree * (degree + 1) / 4.0
    deriv_mat[7, 7] = degree * (degree + 1) / 4.0
    stiffness = deriv_mat.T @ (weights[:, None] * deriv_mat)
    ext_stiff = np.zeros((10, 10))
    ext_stiff[1:9, 1:9] += stiffness
    ext_stiff[0:2, 0:2] += stiffness[6:8, 6:8]
    ext_stiff[8:10, 8:10] += stiffness[0:2, 0:2]
    ext_mass = np.zeros(10)
    ext_mass[1:9] += weights
    ext_mass[0:2] += weights[6:8]
    ext_mass[8:10] += weights[0:2]
    inv_root = 1.0 / np.sqrt(ext_mass)
    eigen_vals, eigen_vecs = jacobi_eigen(inv_root[:, None] * ext_stiff * inv_root[None, :])
    eigen_basis = inv_root[:, None] * eigen_vecs
    return (
        jnp.asarray(stiffness, jnp.float32),
        jnp.asarray(weights, jnp.float32),
        jnp.asarray(eigen_basis, jnp.float32),
        jnp.asarray(eigen_vals, jnp.float32),
    )


def take_rows(widened, low, high, fold_axis):
    return lax.slice_in_dim(widened, low, high, axis=fold_axis)


def face_fold(widened, fold_axis):
    pieces = [
        take_rows(widened, 0, 1, fold_axis),
        take_rows(widened, 2, 3, fold_axis) + take_rows(widened, 1, 2, fold_axis),
        take_rows(widened, 3, 9, fold_axis),
        take_rows(widened, 9, 10, fold_axis) + take_rows(widened, 10, 11, fold_axis),
        take_rows(widened, 11, 12, fold_axis),
    ]
    return jnp.concatenate(pieces, axis=fold_axis)


def spread_fold(widened, fold_axis):
    pieces = [
        take_rows(widened, 3, 5, fold_axis) + take_rows(widened, 0, 2, fold_axis),
        take_rows(widened, 5, 9, fold_axis),
        take_rows(widened, 9, 11, fold_axis) + take_rows(widened, 12, 14, fold_axis),
    ]
    return jnp.concatenate(pieces, axis=fold_axis)


def z_windows(field_in, span):
    leading = field_in.shape[:2]
    elements = field_in.shape[2] // 7
    blocks = jnp.moveaxis(field_in.reshape(leading + (elements, 7)), 2, 3)
    if span == 8:
        return jnp.concatenate([blocks, jnp.roll(blocks[:, :, 0:1], -1, axis=3)], axis=2)
    behind = jnp.roll(blocks[:, :, 6:7], 1, axis=3)
    forward = jnp.roll(blocks[:, :, 0:2], -1, axis=3)
    return jnp.concatenate([behind, blocks, forward], axis=2)


def z_fold(blocks):
    if blocks.shape[2] == 8:
        owned = jnp.concatenate(
            [blocks[:, :, 0:1] + jnp.roll(blocks[:, :, 7:8], 1, axis=3), blocks[:, :, 1:7]], axis=2
        )
    else:
        first_two = blocks[:, :, 1:3] + jnp.roll(blocks[:, :, 8:10], 1, axis=3)
        last_one = blocks[:, :, 7:8] + jnp.roll(blocks[:, :, 0:1], -1, axis=3)
        owned = jnp.concatenate([first_two, blocks[:, :, 3:7], last_one], axis=2)
    leading = owned.shape[:2]
    return jnp.moveaxis(owned, 2, 3).reshape(leading + (-1,))


def element_apply(blocks, stiff_line, mass_line, stiffness, weights):
    along_x = jnp.einsum("ai,ijte->ajte", stiffness, blocks, precision=exact_mode)
    along_y = jnp.einsum("aj,ijte->iate", stiffness, blocks, precision=exact_mode)
    along_z = jnp.einsum("at,ijte->ijae", stiffness, blocks, precision=exact_mode)
    weight_x = weights[:, None, None, None]
    weight_y = weights[None, :, None, None]
    weight_z = weights[None, None, :, None]
    laplace = (
        along_x * weight_y * weight_z
        + along_y * weight_x * weight_z
        + along_z * weight_x * weight_y
    )
    return stiff_line * laplace + mass_line * (weight_x * weight_y * weight_z) * blocks


def local_solve(blocks, stiff_line, mass_line, eigen_basis, eigen_vals):
    spectral = jnp.einsum("ia,ijte->ajte", eigen_basis, blocks, precision=exact_mode)
    spectral = jnp.einsum("jb,ajte->abte", eigen_basis, spectral, precision=exact_mode)
    spectral = jnp.einsum("tc,abte->abce", eigen_basis, spectral, precision=exact_mode)
    eigen_sum = eigen_vals[:, None, None] + eigen_vals[None, :, None] + eigen_vals[None, None, :]
    spectral = spectral / (stiff_line * eigen_sum[..., None] + mass_line)
    restored = jnp.einsum("ai,ijte->ajte", eigen_basis, spectral, precision=exact_mode)
    restored = jnp.einsum("bj,ajte->abte", eigen_basis, restored, precision=exact_mode)
    return jnp.einsum("ct,abte->abce", eigen_basis, restored, precision=exact_mode)


def local(right_side, stiff_coef, mass_coef, coarse_factor):
    stiffness, weights, eigen_basis, eigen_vals = gll_tables()
    stiff_line = stiff_coef.reshape(-1)
    mass_line = mass_coef.reshape(-1)
    z_points = right_side.shape[2]
    coarse_count = coarse_factor.shape[0]

    def widen(field_in):
        widened = with_halo(field_in, (("gx", 0), ("gy", 1)), 2)
        return face_fold(face_fold(widened, 0), 1)

    def operate(direction):
        summed = z_fold(
            element_apply(z_windows(direction, 8), stiff_line, mass_line, stiffness, weights)
        )
        return widen(summed)

    def owned_part(current):
        return current[1:8, 1:8]

    def coarse_total(partial_y):
        summed_rows = partial_y
        rounds = lax.axis_size(("gx", "gy")).bit_length() - 1
        for address_bit in range(rounds):
            summed_rows = summed_rows + swapped(summed_rows, ("gx", "gy"), address_bit)
        return summed_rows

    def precondition(extended):
        summed = z_fold(
            local_solve(z_windows(extended, 10), stiff_line, mass_line, eigen_basis, eigen_vals)
        )
        widened = with_halo(summed, (("gx", 0), ("gy", 1)), 2)
        smooth = spread_fold(spread_fold(widened, 0), 1)
        coarse_in = jnp.sum(extended[2:8, 2:8], axis=(0, 1)).reshape(coarse_count, -1).sum(axis=1)
        partial_y = jnp.dot(coarse_in, coarse_factor, precision=exact_mode)
        coarse_out = jnp.dot(coarse_factor, coarse_total(partial_y), precision=exact_mode)
        coarse_line = jnp.broadcast_to(
            coarse_out[:, None], (coarse_count, z_points // coarse_count)
        ).reshape(-1)
        coarse_plate = jnp.pad(
            jnp.broadcast_to(coarse_line, (6, 6, z_points)), ((1, 1), (1, 1), (0, 0))
        )
        return smooth + coarse_plate

    def global_pair(current, smooth, applied):
        return lax.psum(
            (
                jnp.sum(owned_part(current) * smooth[:7, :7]),
                jnp.sum(smooth[:7, :7] * owned_part(applied)),
            ),
            ("gx", "gy"),
        )

    current = widen(jnp.pad(right_side, ((0, 1), (0, 1), (0, 0))))
    solution = jnp.zeros(right_side.shape, jnp.float32)
    smooth = precondition(current)
    applied = operate(smooth)
    rho_now, curvature = global_pair(current, smooth, applied)
    step_len = rho_now / curvature
    direction, applied_dir = (smooth, applied)
    for iteration in range(ITERS):
        solution = solution + step_len * direction[:7, :7]
        current = current - step_len * applied_dir
        if iteration + 1 < ITERS:
            smooth = precondition(current)
            applied = operate(smooth)
            rho_next, curvature = global_pair(current, smooth, applied)
            momentum = rho_next / rho_now
            step_len = rho_next / (curvature - momentum * rho_next / step_len)
            direction = smooth + momentum * direction
            applied_dir = applied + momentum * applied_dir
            rho_now = rho_next
    return (solution, owned_part(current))


def solution(mesh):
    placed = (P("gx", "gy", None), P("gx", "gy", None), P("gx", "gy", None), P(("gx", "gy"), None))
    return jax.shard_map(
        local,
        mesh=mesh,
        in_specs=placed,
        out_specs=(P("gx", "gy", None), P("gx", "gy", None)),
        check_vma=False,
    )
```

profile of v0, /device:TPU:0, one launch (start us, length us, event | category | flops | bytes accessed | tf_op | source)
XLA Modules:
  0.0 204.7 jit_solution(3485717478695533457)
XLA Ops:
  3.0 2.5 %collective-permute-start = (f32[2,8,168]{2,1,0:T(8,128)S(1)}, f32[2,8,168]{2,1,0:T(8,128)S(1)}, u32[]{:S(2)}, u32[]{:S(2)}) collective-permute-start(f32[2,8,168]{2,1,0:T(8,128)S(1)} %get-tuple-element.68), channel_id=1, source_target_pairs={{0,8},{8,16},{16,24},{24,0},{1,9},{9,17},{17,25},{25,1},{2,10},{10... | collective-permute-start | bytes 32264 | tf_op jit(solution)/shard_map/ppermute | solution.py:21
  6.5 2.0 collective-permute-start.9
  10.1 3.0 %collective-permute-start.10 = (f32[256]{0:T(256)S(1)}, f32[256]{0:T(256)S(1)}, u32[]{:S(2)}, u32[]{:S(2)}) collective-permute-start(f32[256]{0:T(256)S(1)} %add.238), channel_id=1, source_target_pairs={{0,4},{1,5},{2,6},{3,7},{4,0},{5,1},{6,2},{7,3},{8,12},{9,13},{10,... | collective-permute-start | bytes 3080 | tf_op jit(solution)/shard_map/ppermute | solution.py:30
  16.4 1.8 collective-permute-done.11
  18.2 1.9 collective-permute-start.12
  21.9 3.5 %collective-permute-start.3 = (f32[12,2,168]{2,1,0:T(2,128)S(1)}, f32[12,2,168]{2,1,0:T(2,128)S(1)}, u32[]{:S(2)}, u32[]{:S(2)}) collective-permute-start(f32[12,2,168]{2,1,0:T(2,128)S(1)} %get-tuple-element.67), channel_id=1, source_target_pairs={{1,0},{2,1},{3,2},{4,3},{5,4},{6,5},{7,6},{0,7},{9,8},{10,9},{11,1... | collective-permute-start | bytes 48392 | tf_op jit(solution)/shard_map/ppermute | solution.py:24
  25.7 1.2 collective-permute-done.2
  27.8 1.2 copy.146
  39.8 2.0 collective-permute-start.5
  42.3 1.8 collective-permute-done.5
  44.2 3.5 %collective-permute-start.7 = (f32[14,2,168]{2,1,0:T(2,128)S(1)}, f32[14,2,168]{2,1,0:T(2,128)S(1)}, u32[]{:S(2)}, u32[]{:S(2)}) collective-permute-start(f32[14,2,168]{2,1,0:T(2,128)S(1)} %get-tuple-element.37), channel_id=1, source_target_pairs={{1,0},{2,1},{3,2},{4,3},{5,4},{6,5},{7,6},{0,7},{9,8},{10,9},{11,1... | collective-permute-start | bytes 56456 | tf_op jit(solution)/shard_map/ppermute | solution.py:24
  52.5 3.0 %collective-permute-start.13 = (f32[2,8,168]{2,1,0:T(8,128)S(1)}, f32[2,8,168]{2,1,0:T(8,128)S(1)}, u32[]{:S(2)}, u32[]{:S(2)}) collective-permute-start(f32[2,8,168]{2,1,0:T(8,128)S(1)} %slice.517), channel_id=1, source_target_pairs={{0,8},{8,16},{16,24},{24,0},{1,9},{9,17},{17,25},{25,1},{2,10},{10... | collective-permute-start | bytes 32264 | tf_op jit(solution)/shard_map/ppermute | solution.py:21
  57.3 3.0 %collective-permute-done.14 = f32[2,8,168]{2,1,0:T(8,128)S(1)} collective-permute-done((f32[2,8,168]{2,1,0:T(8,128)S(1)}, f32[2,8,168]{2,1,0:T(8,128)S(1)}, u32[]{:S(2)}, u32[]{:S(2)}) %collective-permute-start.14) | collective-permute-done | bytes 10784 | tf_op jit(solution)/shard_map/ppermute | solution.py:24
  60.5 3.5 %collective-permute-start.16 = (f32[12,2,168]{2,1,0:T(2,128)S(1)}, f32[12,2,168]{2,1,0:T(2,128)S(1)}, u32[]{:S(2)}, u32[]{:S(2)}) collective-permute-start(f32[12,2,168]{2,1,0:T(2,128)S(1)} %get-tuple-element.65), channel_id=1, source_target_pairs={{1,0},{2,1},{3,2},{4,3},{5,4},{6,5},{7,6},{0,7},{9,8},{10,9},{11,1... | collective-permute-start | bytes 48392 | tf_op jit(solution)/shard_map/ppermute | solution.py:24
  68.8 38.5 %all-reduce.4 = (f32[]{:T(128)}, f32[]{:T(128)}) all-reduce(f32[]{:T(128)} %get-tuple-element.9, f32[]{:T(128)} %get-tuple-element.8), channel_id=1, replica_groups=mesh['gx'=4,'gy'=8] {'gx','gy'}, use_global_device_ids=true, to_apply=%region_3.4 | all-reduce | flops 2 | bytes 16 | tf_op jit(solution)/shard_map/psum | solution.py:239
  117.1 2.3 %collective-permute-start.17 = (f32[2,10,168]{2,1,0:T(8,128)S(1)}, f32[2,10,168]{2,1,0:T(8,128)S(1)}, u32[]{:S(2)}, u32[]{:S(2)}) collective-permute-start(f32[2,10,168]{2,1,0:T(8,128)S(1)} %reshape.156), channel_id=1, source_target_pairs={{0,8},{8,16},{16,24},{24,0},{1,9},{9,17},{17,25},{25,1},{2,10},{10... | collective-permute-start | bytes 40328 | tf_op jit(solution)/shard_map/ppermute | solution.py:21
  120.7 2.1 %collective-permute-start.22 = (f32[256]{0:T(256)S(1)}, f32[256]{0:T(256)S(1)}, u32[]{:S(2)}, u32[]{:S(2)}) collective-permute-start(f32[256]{0:T(256)S(1)} %add.257), channel_id=1, source_target_pairs={{0,2},{1,3},{2,0},{3,1},{4,6},{5,7},{6,4},{7,5},{8,10},{9,11},{10,... | collective-permute-start | bytes 3080 | tf_op jit(solution)/shard_map/ppermute | solution.py:30
  122.9 1.5 collective-permute-done.22
  124.4 2.8 %collective-permute-start.23 = (f32[256]{0:T(256)S(1)}, f32[256]{0:T(256)S(1)}, u32[]{:S(2)}, u32[]{:S(2)}) collective-permute-start(f32[256]{0:T(256)S(1)} %add.258), channel_id=1, source_target_pairs={{0,4},{1,5},{2,6},{3,7},{4,0},{5,1},{6,2},{7,3},{8,12},{9,13},{10,... | collective-permute-start | bytes 3080 | tf_op jit(solution)/shard_map/ppermute | solution.py:30
  127.2 1.6 collective-permute-done.23
  128.9 1.7 collective-permute-start.24
  130.5 1.9 collective-permute-done.24
  132.4 1.3 collective-permute-start.25
  134.8 1.8 collective-permute-start.18
  137.1 1.7 collective-permute-done.18
  138.8 3.5 %collective-permute-start.20 = (f32[14,2,168]{2,1,0:T(2,128)S(1)}, f32[14,2,168]{2,1,0:T(2,128)S(1)}, u32[]{:S(2)}, u32[]{:S(2)}) collective-permute-start(f32[14,2,168]{2,1,0:T(2,128)S(1)} %get-tuple-element.33), channel_id=1, source_target_pairs={{1,0},{2,1},{3,2},{4,3},{5,4},{6,5},{7,6},{0,7},{9,8},{10,9},{11,1... | collective-permute-start | bytes 56456 | tf_op jit(solution)/shard_map/ppermute | solution.py:24
  142.7 1.3 collective-permute-done.19
  147.6 1.3 collective-permute-start.26
  149.6 1.8 collective-permute-start.27
  153.4 3.5 %collective-permute-start.29 = (f32[12,2,168]{2,1,0:T(2,128)S(1)}, f32[12,2,168]{2,1,0:T(2,128)S(1)}, u32[]{:S(2)}, u32[]{:S(2)}) collective-permute-start(f32[12,2,168]{2,1,0:T(2,128)S(1)} %get-tuple-element.63), channel_id=1, source_target_pairs={{1,0},{2,1},{3,2},{4,3},{5,4},{6,5},{7,6},{0,7},{9,8},{10,9},{11,1... | collective-permute-start | bytes 48392 | tf_op jit(solution)/shard_map/ppermute | solution.py:24
  157.0 1.5 collective-permute-done.28
  159.4 39.5 %all-reduce.3 = (f32[]{:T(128)}, f32[]{:T(128)}) all-reduce(f32[]{:T(128)} %get-tuple-element.7, f32[]{:T(128)} %get-tuple-element.6), channel_id=1, replica_groups=mesh['gx'=4,'gy'=8] {'gx','gy'}, use_global_device_ids=true, to_apply=%region_9.10 | all-reduce | flops 2 | bytes 16 | tf_op jit(solution)/shard_map/psum | solution.py:239
  (257 shorter events, 53.3 us)
Async XLA Ops:
  1.8 4.7 %collective-permute-start.8 = (f32[256]{0:T(256)S(1)}, f32[256]{0:T(256)S(1)}, u32[]{:S(2)}, u32[]{:S(2)}) collective-permute-start(f32[256]{0:T(256)S(1)} %bitcast.153), channel_id=1, source_target_pairs={{0,1},{1,0},{2,3},{3,2},{4,5},{5,4},{6,7},{7,6},{8,9},{9,8},{10,11... | collective-permute-start | bytes 3080 | tf_op jit(solution)/shard_map/ppermute | solution.py:30
  3.0 18.8 %collective-permute-start = (f32[2,8,168]{2,1,0:T(8,128)S(1)}, f32[2,8,168]{2,1,0:T(8,128)S(1)}, u32[]{:S(2)}, u32[]{:S(2)}) collective-permute-start(f32[2,8,168]{2,1,0:T(8,128)S(1)} %get-tuple-element.68), channel_id=1, source_target_pairs={{0,8},{8,16},{16,24},{24,0},{1,9},{9,17},{17,25},{25,1},{2,10},{10... | collective-permute-start | bytes 32264 | tf_op jit(solution)/shard_map/ppermute | solution.py:21
  5.5 16.3 %collective-permute-start.1 = (f32[2,8,168]{2,1,0:T(8,128)S(1)}, f32[2,8,168]{2,1,0:T(8,128)S(1)}, u32[]{:S(2)}, u32[]{:S(2)}) collective-permute-start(f32[2,8,168]{2,1,0:T(8,128)S(1)} %get-tuple-element.69), channel_id=1, source_target_pairs={{8,0},{16,8},{24,16},{0,24},{9,1},{17,9},{25,17},{1,25},{10,2},{18... | collective-permute-start | bytes 32264 | tf_op jit(solution)/shard_map/ppermute | solution.py:24
  6.5 3.6 %collective-permute-start.9 = (f32[256]{0:T(256)S(1)}, f32[256]{0:T(256)S(1)}, u32[]{:S(2)}, u32[]{:S(2)}) collective-permute-start(f32[256]{0:T(256)S(1)} %add.237), channel_id=1, source_target_pairs={{0,2},{1,3},{2,0},{3,1},{4,6},{5,7},{6,4},{7,5},{8,10},{9,11},{10,... | collective-permute-start | bytes 3080 | tf_op jit(solution)/shard_map/ppermute | solution.py:30
  10.1 4.6 %collective-permute-start.10 = (f32[256]{0:T(256)S(1)}, f32[256]{0:T(256)S(1)}, u32[]{:S(2)}, u32[]{:S(2)}) collective-permute-start(f32[256]{0:T(256)S(1)} %add.238), channel_id=1, source_target_pairs={{0,4},{1,5},{2,6},{3,7},{4,0},{5,1},{6,2},{7,3},{8,12},{9,13},{10,... | collective-permute-start | bytes 3080 | tf_op jit(solution)/shard_map/ppermute | solution.py:30
  14.7 3.6 %collective-permute-start.11 = (f32[256]{0:T(256)S(1)}, f32[256]{0:T(256)S(1)}, u32[]{:S(2)}, u32[]{:S(2)}) collective-permute-start(f32[256]{0:T(256)S(1)} %add.239), channel_id=1, source_target_pairs={{0,8},{1,9},{2,10},{3,11},{4,12},{5,13},{6,14},{7,15},{8,0},{9,1},... | collective-permute-start | bytes 3080 | tf_op jit(solution)/shard_map/ppermute | solution.py:30
  18.2 3.6 %collective-permute-start.12 = (f32[256]{0:T(256)S(1)}, f32[256]{0:T(256)S(1)}, u32[]{:S(2)}, u32[]{:S(2)}) collective-permute-start(f32[256]{0:T(256)S(1)} %add.240), channel_id=1, source_target_pairs={{0,16},{1,17},{2,18},{3,19},{4,20},{5,21},{6,22},{7,23},{8,24},{9,... | collective-permute-start | bytes 3080 | tf_op jit(solution)/shard_map/ppermute | solution.py:30
  21.8 5.1 %collective-permute-start.2 = (f32[12,2,168]{2,1,0:T(2,128)S(1)}, f32[12,2,168]{2,1,0:T(2,128)S(1)}, u32[]{:S(2)}, u32[]{:S(2)}) collective-permute-start(f32[12,2,168]{2,1,0:T(2,128)S(1)} %get-tuple-element.66), channel_id=1, source_target_pairs={{0,1},{1,2},{2,3},{3,4},{4,5},{5,6},{6,7},{7,0},{8,9},{9,10},{10,1... | collective-permute-start | bytes 48392 | tf_op jit(solution)/shard_map/ppermute | solution.py:21
  21.9 5.1 %collective-permute-start.3 = (f32[12,2,168]{2,1,0:T(2,128)S(1)}, f32[12,2,168]{2,1,0:T(2,128)S(1)}, u32[]{:S(2)}, u32[]{:S(2)}) collective-permute-start(f32[12,2,168]{2,1,0:T(2,128)S(1)} %get-tuple-element.67), channel_id=1, source_target_pairs={{1,0},{2,1},{3,2},{4,3},{5,4},{6,5},{7,6},{0,7},{9,8},{10,9},{11,1... | collective-permute-start | bytes 48392 | tf_op jit(solution)/shard_map/ppermute | solution.py:24
  27.8 1.5 copy-start.1
  37.5 4.7 %collective-permute-start.4 = (f32[2,10,168]{2,0,1:T(2,128)S(1)}, f32[2,10,168]{2,0,1:T(2,128)S(1)}, u32[]{:S(2)}, u32[]{:S(2)}) collective-permute-start(f32[2,10,168]{2,0,1:T(2,128)S(1)} %slice.493), channel_id=1, source_target_pairs={{0,8},{8,16},{16,24},{24,0},{1,9},{9,17},{17,25},{25,1},{2,10},{10... | collective-permute-start | bytes 40328 | tf_op jit(solution)/shard_map/ppermute | solution.py:21
  39.8 4.3 %collective-permute-start.5 = (f32[2,10,168]{2,1,0:T(8,128)S(1)}, f32[2,10,168]{2,1,0:T(8,128)S(1)}, u32[]{:S(2)}, u32[]{:S(2)}) collective-permute-start(f32[2,10,168]{2,1,0:T(8,128)S(1)} %reshape.155), channel_id=1, source_target_pairs={{8,0},{16,8},{24,16},{0,24},{9,1},{17,9},{25,17},{1,25},{10,2},{18... | collective-permute-start | bytes 40328 | tf_op jit(solution)/shard_map/ppermute | solution.py:24
  44.1 5.2 %collective-permute-start.6 = (f32[14,2,168]{2,1,0:T(2,128)S(1)}, f32[14,2,168]{2,1,0:T(2,128)S(1)}, u32[]{:S(2)}, u32[]{:S(2)}) collective-permute-start(f32[14,2,168]{2,1,0:T(2,128)S(1)} %get-tuple-element.36), channel_id=1, source_target_pairs={{0,1},{1,2},{2,3},{3,4},{4,5},{5,6},{6,7},{7,0},{8,9},{9,10},{10,1... | collective-permute-start | bytes 56456 | tf_op jit(solution)/shard_map/ppermute | solution.py:21
  44.2 5.1 %collective-permute-start.7 = (f32[14,2,168]{2,1,0:T(2,128)S(1)}, f32[14,2,168]{2,1,0:T(2,128)S(1)}, u32[]{:S(2)}, u32[]{:S(2)}) collective-permute-start(f32[14,2,168]{2,1,0:T(2,128)S(1)} %get-tuple-element.37), channel_id=1, source_target_pairs={{1,0},{2,1},{3,2},{4,3},{5,4},{6,5},{7,6},{0,7},{9,8},{10,9},{11,1... | collective-permute-start | bytes 56456 | tf_op jit(solution)/shard_map/ppermute | solution.py:24
  49.8 1.6 copy-start.3
  52.5 4.8 %collective-permute-start.13 = (f32[2,8,168]{2,1,0:T(8,128)S(1)}, f32[2,8,168]{2,1,0:T(8,128)S(1)}, u32[]{:S(2)}, u32[]{:S(2)}) collective-permute-start(f32[2,8,168]{2,1,0:T(8,128)S(1)} %slice.517), channel_id=1, source_target_pairs={{0,8},{8,16},{16,24},{24,0},{1,9},{9,17},{17,25},{25,1},{2,10},{10... | collective-permute-start | bytes 32264 | tf_op jit(solution)/shard_map/ppermute | solution.py:21
  56.6 3.8 %collective-permute-start.14 = (f32[2,8,168]{2,1,0:T(8,128)S(1)}, f32[2,8,168]{2,1,0:T(8,128)S(1)}, u32[]{:S(2)}, u32[]{:S(2)}) collective-permute-start(f32[2,8,168]{2,1,0:T(8,128)S(1)} %slice.519), channel_id=1, source_target_pairs={{8,0},{16,8},{24,16},{0,24},{9,1},{17,9},{25,17},{1,25},{10,2},{18... | collective-permute-start | bytes 32264 | tf_op jit(solution)/shard_map/ppermute | solution.py:24
  60.4 5.1 %collective-permute-start.15 = (f32[12,2,168]{2,1,0:T(2,128)S(1)}, f32[12,2,168]{2,1,0:T(2,128)S(1)}, u32[]{:S(2)}, u32[]{:S(2)}) collective-permute-start(f32[12,2,168]{2,1,0:T(2,128)S(1)} %get-tuple-element.64), channel_id=1, source_target_pairs={{0,1},{1,2},{2,3},{3,4},{4,5},{5,6},{6,7},{7,0},{8,9},{9,10},{10,1... | collective-permute-start | bytes 48392 | tf_op jit(solution)/shard_map/ppermute | solution.py:21
  60.5 5.1 %collective-permute-start.16 = (f32[12,2,168]{2,1,0:T(2,128)S(1)}, f32[12,2,168]{2,1,0:T(2,128)S(1)}, u32[]{:S(2)}, u32[]{:S(2)}) collective-permute-start(f32[12,2,168]{2,1,0:T(2,128)S(1)} %get-tuple-element.65), channel_id=1, source_target_pairs={{1,0},{2,1},{3,2},{4,3},{5,4},{6,5},{7,6},{0,7},{9,8},{10,9},{11,1... | collective-permute-start | bytes 48392 | tf_op jit(solution)/shard_map/ppermute | solution.py:24
  117.1 19.9 %collective-permute-start.17 = (f32[2,10,168]{2,1,0:T(8,128)S(1)}, f32[2,10,168]{2,1,0:T(8,128)S(1)}, u32[]{:S(2)}, u32[]{:S(2)}) collective-permute-start(f32[2,10,168]{2,1,0:T(8,128)S(1)} %reshape.156), channel_id=1, source_target_pairs={{0,8},{8,16},{16,24},{24,0},{1,9},{9,17},{17,25},{25,1},{2,10},{10... | collective-permute-start | bytes 40328 | tf_op jit(solution)/shard_map/ppermute | solution.py:21
  119.6 1.1 collective-permute-start.21
  120.7 3.7 %collective-permute-start.22 = (f32[256]{0:T(256)S(1)}, f32[256]{0:T(256)S(1)}, u32[]{:S(2)}, u32[]{:S(2)}) collective-permute-start(f32[256]{0:T(256)S(1)} %add.257), channel_id=1, source_target_pairs={{0,2},{1,3},{2,0},{3,1},{4,6},{5,7},{6,4},{7,5},{8,10},{9,11},{10,... | collective-permute-start | bytes 3080 | tf_op jit(solution)/shard_map/ppermute | solution.py:30
  124.4 4.5 %collective-permute-start.23 = (f32[256]{0:T(256)S(1)}, f32[256]{0:T(256)S(1)}, u32[]{:S(2)}, u32[]{:S(2)}) collective-permute-start(f32[256]{0:T(256)S(1)} %add.258), channel_id=1, source_target_pairs={{0,4},{1,5},{2,6},{3,7},{4,0},{5,1},{6,2},{7,3},{8,12},{9,13},{10,... | collective-permute-start | bytes 3080 | tf_op jit(solution)/shard_map/ppermute | solution.py:30
  128.9 3.6 %collective-permute-start.24 = (f32[256]{0:T(256)S(1)}, f32[256]{0:T(256)S(1)}, u32[]{:S(2)}, u32[]{:S(2)}) collective-permute-start(f32[256]{0:T(256)S(1)} %add.259), channel_id=1, source_target_pairs={{0,8},{1,9},{2,10},{3,11},{4,12},{5,13},{6,14},{7,15},{8,0},{9,1},... | collective-permute-start | bytes 3080 | tf_op jit(solution)/shard_map/ppermute | solution.py:30
  132.4 4.6 %collective-permute-start.25 = (f32[256]{0:T(256)S(1)}, f32[256]{0:T(256)S(1)}, u32[]{:S(2)}, u32[]{:S(2)}) collective-permute-start(f32[256]{0:T(256)S(1)} %add.260), channel_id=1, source_target_pairs={{0,16},{1,17},{2,18},{3,19},{4,20},{5,21},{6,22},{7,23},{8,24},{9,... | collective-permute-start | bytes 3080 | tf_op jit(solution)/shard_map/ppermute | solution.py:30
  134.8 4.0 %collective-permute-start.18 = (f32[2,10,168]{2,1,0:T(8,128)S(1)}, f32[2,10,168]{2,1,0:T(8,128)S(1)}, u32[]{:S(2)}, u32[]{:S(2)}) collective-permute-start(f32[2,10,168]{2,1,0:T(8,128)S(1)} %reshape.157), channel_id=1, source_target_pairs={{8,0},{16,8},{24,16},{0,24},{9,1},{17,9},{25,17},{1,25},{10,2},{18... | collective-permute-start | bytes 40328 | tf_op jit(solution)/shard_map/ppermute | solution.py:24
  138.8 5.1 %collective-permute-start.19 = (f32[14,2,168]{2,1,0:T(2,128)S(1)}, f32[14,2,168]{2,1,0:T(2,128)S(1)}, u32[]{:S(2)}, u32[]{:S(2)}) collective-permute-start(f32[14,2,168]{2,1,0:T(2,128)S(1)} %get-tuple-element.32), channel_id=1, source_target_pairs={{0,1},{1,2},{2,3},{3,4},{4,5},{5,6},{6,7},{7,0},{8,9},{9,10},{10,1... | collective-permute-start | bytes 56456 | tf_op jit(solution)/shard_map/ppermute | solution.py:21
  138.8 5.1 %collective-permute-start.20 = (f32[14,2,168]{2,1,0:T(2,128)S(1)}, f32[14,2,168]{2,1,0:T(2,128)S(1)}, u32[]{:S(2)}, u32[]{:S(2)}) collective-permute-start(f32[14,2,168]{2,1,0:T(2,128)S(1)} %get-tuple-element.33), channel_id=1, source_target_pairs={{1,0},{2,1},{3,2},{4,3},{5,4},{6,5},{7,6},{0,7},{9,8},{10,9},{11,1... | collective-permute-start | bytes 56456 | tf_op jit(solution)/shard_map/ppermute | solution.py:24
  147.6 4.7 %collective-permute-start.26 = (f32[2,8,168]{2,1,0:T(8,128)S(1)}, f32[2,8,168]{2,1,0:T(8,128)S(1)}, u32[]{:S(2)}, u32[]{:S(2)}) collective-permute-start(f32[2,8,168]{2,1,0:T(8,128)S(1)} %slice.574), channel_id=1, source_target_pairs={{0,8},{8,16},{16,24},{24,0},{1,9},{9,17},{17,25},{25,1},{2,10},{10... | collective-permute-start | bytes 32264 | tf_op jit(solution)/shard_map/ppermute | solution.py:21
  149.6 3.8 %collective-permute-start.27 = (f32[2,8,168]{2,1,0:T(8,128)S(1)}, f32[2,8,168]{2,1,0:T(8,128)S(1)}, u32[]{:S(2)}, u32[]{:S(2)}) collective-permute-start(f32[2,8,168]{2,1,0:T(8,128)S(1)} %slice.576), channel_id=1, source_target_pairs={{8,0},{16,8},{24,16},{0,24},{9,1},{17,9},{25,17},{1,25},{10,2},{18... | collective-permute-start | bytes 32264 | tf_op jit(solution)/shard_map/ppermute | solution.py:24
  153.4 5.1 %collective-permute-start.28 = (f32[12,2,168]{2,1,0:T(2,128)S(1)}, f32[12,2,168]{2,1,0:T(2,128)S(1)}, u32[]{:S(2)}, u32[]{:S(2)}) collective-permute-start(f32[12,2,168]{2,1,0:T(2,128)S(1)} %get-tuple-element.62), channel_id=1, source_target_pairs={{0,1},{1,2},{2,3},{3,4},{4,5},{5,6},{6,7},{7,0},{8,9},{9,10},{10,1... | collective-permute-start | bytes 48392 | tf_op jit(solution)/shard_map/ppermute | solution.py:21
  153.4 5.1 %collective-permute-start.29 = (f32[12,2,168]{2,1,0:T(2,128)S(1)}, f32[12,2,168]{2,1,0:T(2,128)S(1)}, u32[]{:S(2)}, u32[]{:S(2)}) collective-permute-start(f32[12,2,168]{2,1,0:T(2,128)S(1)} %get-tuple-element.63), channel_id=1, source_target_pairs={{1,0},{2,1},{3,2},{4,3},{5,4},{6,5},{7,6},{0,7},{9,8},{10,9},{11,1... | collective-permute-start | bytes 48392 | tf_op jit(solution)/shard_map/ppermute | solution.py:24
  (4 other events, 4.5 us)
where the time goes:
time: 206 us; the launch traced here: 205 us
  blocking collectives  78 us (38%)
  starting transfers between devices  50.9 us (25%)
  waiting for transfers between devices  24.3 us (12%)
  local copies, waits for them, and re-layouts  18.1 us (9%)
  matrix products  16 us (8%)
  other arithmetic  9.91 us (5%)
  between operations  7.53 us (4%)
    psum x2, blocking collectives, global_pair(): lax.psum((jnp.sum(owned_part(current) * smooth[:7, :7]), jnp.sum(smooth[:...  78 us
    ppermute x10, starting transfers between devices, with_halo(): lax.ppermute(lax.slice_in_dim(block, 0, width, axis=dim), axis, backward)  24.3 us
    ppermute x10, starting transfers between devices, swapped(): lax.ppermute(shard, axis, [(i, i ^ 1 << apart) for i in range(lax.axis_si...  16.2 us
    ppermute x10, starting transfers between devices, with_halo(): lax.ppermute(lax.slice_in_dim(block, block.shape[dim] - width, None, axis...  10.3 us
    ppermute x10, waiting for transfers between devices, swapped(): lax.ppermute(shard, axis, [(i, i ^ 1 << apart) for i in range(lax.axis_si...  9.82 us
    ppermute x10, waiting for transfers between devices, with_halo(): lax.ppermute(lax.slice_in_dim(block, 0, width, axis=dim), axis, backward)  7.71 us
    ppermute x10, waiting for transfers between devices, with_halo(): lax.ppermute(lax.slice_in_dim(block, block.shape[dim] - width, None, axis...  6.77 us
    concatenate x24, local copies, waits for them, and re-layouts, face_fold(): return jnp.concatenate(pieces, axis=fold_axis)  4.72 us
  transfers between devices with their start and end apart: 30, of which 19 were waited for; matrix products, arithmetic and copies ran while one was open for 6% of the time, Pallas kernels for 0%

commit v1 on v0

v1 whole, which is shorter than its diff:
```python
import functools
import math

import jax
import jax.numpy as jnp
import numpy as np
from jax import lax
from jax.experimental import pallas as pl
from jax.experimental.pallas import tpu as pltpu
from jax.sharding import PartitionSpec as P

MESH = pl.DeviceIdType.MESH
exact_mode = lax.Precision.HIGHEST
ROUNDS = 5

OWN = 64
SLOTS = (
    (-1, 0, 64, 16),
    (1, 0, 80, 16),
    (0, -1, 96, 16),
    (0, 1, 112, 16),
    (-1, -1, 128, 8),
    (-1, 1, 136, 8),
    (1, -1, 144, 8),
    (1, 1, 152, 8),
)
STACK = 160
SPEC = 112


def legendre_pair(position, degree):
    p_prev = 1.0
    p_now = position
    for order in range(2, degree + 1):
        p_next = ((2 * order - 1) * position * p_now - (order - 1) * p_prev) / order
        p_prev = p_now
        p_now = p_next
    return (p_now, p_prev)


def jacobi_eigen(matrix):
    size_n = matrix.shape[0]
    current = np.array(matrix)
    vectors = np.eye(size_n)
    for sweep in range(20):
        for row_p in range(size_n - 1):
            for row_q in range(row_p + 1, size_n):
                off_value = current[row_p, row_q]
                if abs(off_value) > 1e-300:
                    theta = (current[row_q, row_q] - current[row_p, row_p]) / (2.0 * off_value)
                    sign_t = 1.0 if theta >= 0.0 else -1.0
                    tangent = sign_t / (abs(theta) + math.sqrt(theta * theta + 1.0))
                    cosine = 1.0 / math.sqrt(tangent * tangent + 1.0)
                    sine = tangent * cosine
                    rotation = np.eye(size_n)
                    rotation[row_p, row_p] = cosine
                    rotation[row_q, row_q] = cosine
                    rotation[row_p, row_q] = sine
                    rotation[row_q, row_p] = -sine
                    current = rotation.T @ current @ rotation
                    vectors = vectors @ rotation
    return (np.array([current[idx, idx] for idx in range(size_n)]), vectors)


def gll_tables():
    degree = 7
    guesses = [
        -0.8717401485096066,
        -0.5917001814331423,
        -0.2092992179024789,
        0.2092992179024789,
        0.5917001814331423,
        0.8717401485096066,
    ]
    interior = []
    for guess in guesses:
        position = guess
        for newton in range(30):
            p_now, p_prev = legendre_pair(position, degree)
            first = degree * (position * p_now - p_prev) / (position * position - 1.0)
            second = (2.0 * position * first - degree * (degree + 1) * p_now) / (
                1.0 - position * position
            )
            position = position - first / second
        interior.append(position)
    points = np.array([-1.0] + interior + [1.0])
    values = np.array([legendre_pair(float(pt), degree)[0] for pt in points])
    weights = 2.0 / (degree * (degree + 1) * values**2)
    deriv_mat = np.zeros((8, 8))
    for left_idx in range(8):
        for right_idx in range(8):
            if left_idx != right_idx:
                deriv_mat[left_idx, right_idx] = values[left_idx] / (
                    values[right_idx] * (points[left_idx] - points[right_idx])
                )
    deriv_mat[0, 0] = -degree * (degree + 1) / 4.0
    deriv_mat[7, 7] = degree * (degree + 1) / 4.0
    stiffness = deriv_mat.T @ (weights[:, None] * deriv_mat)
    ext_stiff = np.zeros((10, 10))
    ext_stiff[1:9, 1:9] += stiffness
    ext_stiff[0:2, 0:2] += stiffness[6:8, 6:8]
    ext_stiff[8:10, 8:10] += stiffness[0:2, 0:2]
    ext_mass = np.zeros(10)
    ext_mass[1:9] += weights
    ext_mass[0:2] += weights[6:8]
    ext_mass[8:10] += weights[0:2]
    inv_root = 1.0 / np.sqrt(ext_mass)
    eigen_vals, eigen_vecs = jacobi_eigen(inv_root[:, None] * ext_stiff * inv_root[None, :])
    eigen_basis = inv_root[:, None] * eigen_vecs
    return stiffness, weights, eigen_basis, eigen_vals


def round_up(count, unit):
    return -(-count // unit) * unit


def stack_map(taken, placed, size_from, size_to):
    pick = np.zeros((STACK, size_from * size_from))
    place = np.zeros((size_to * size_to, STACK))
    for off_x, off_y, start, _ in ((0, 0, 0, OWN),) + SLOTS:
        row = start
        for from_x, to_x in zip(taken[off_x], placed[off_x]):
            for from_y, to_y in zip(taken[off_y], placed[off_y]):
                pick[row, from_x * size_from + from_y] = 1.0
                place[to_x * size_to + to_y, row] = 1.0
                row += 1
    return pick, place


def halves(matrix):
    exact = np.asarray(matrix, np.float32)
    high = exact.astype(jnp.bfloat16)
    low = (exact - high.astype(np.float32)).astype(jnp.bfloat16)
    return high, low


def left_split(matrix):
    high, low = halves(matrix)
    return np.concatenate([high, low, high], axis=1)


def left_exact(matrix):
    return np.concatenate([np.asarray(matrix).astype(jnp.bfloat16)] * 3, axis=1)


def constants(elements, coarse_count):
    stiffness, weights, basis, lam = gll_tables()
    stiffness = np.asarray(stiffness, np.float32).astype(np.float64)
    weights = np.asarray(weights, np.float32).astype(np.float64)
    basis = np.asarray(basis, np.float32).astype(np.float64)
    lam = np.asarray(lam, np.float32).astype(np.float64)
    points = 7 * elements
    z_pad = round_up(points, 128)
    s_pad = round_up(10 * elements, 128)
    every = list(range(8))
    pick_a, place_a = stack_map(
        {-1: [6, 7], 0: every, 1: [0, 1]}, {-1: [0, 1], 0: list(range(1, 9)), 1: [8, 9]}, 8, 10
    )
    pick_s, place_s = stack_map(
        {-1: [8, 9], 0: list(range(1, 9)), 1: [0, 1]}, {-1: [0, 1], 0: every, 1: [6, 7]}, 10, 8
    )
    basis_two = np.kron(basis, basis)
    spectral_in = np.zeros((SPEC, STACK))
    spectral_in[:100] = basis_two.T @ place_a
    spectral_out = np.zeros((STACK, SPEC))
    spectral_out[:, :100] = pick_s @ basis_two
    plane = np.kron(stiffness, np.diag(weights)) + np.kron(np.diag(weights), stiffness)
    plane_weight = np.kron(weights, weights)
    window = np.zeros((z_pad, s_pad))
    own_cols = np.zeros((z_pad, z_pad))
    before_cols = np.zeros((z_pad, z_pad))
    spread = np.zeros((elements, s_pad + 2 * z_pad))
    lines = np.zeros((8, max(z_pad, s_pad)))
    lines[2, 10 * elements :] = 1.0
    for elem in range(elements):
        prior = (elem - 1) % elements
        for col in range(10):
            spread[elem, col * elements + elem] = 1.0
            for row in range(10):
                window[(7 * elem - 1 + row) % points, col * elements + elem] += basis[row, col]
        for step in range(7):
            spread[elem, s_pad + 7 * elem + step] = 1.0
            spread[prior, s_pad + z_pad + 7 * elem + step] = 1.0
            lines[0, 7 * elem + step] = weights[step]
            for row in range(8):
                own_cols[(7 * elem + row) % points, 7 * elem + step] += stiffness[row, step]
        lines[1, 7 * elem] = weights[7]
        for row in range(8):
            before_cols[(7 * prior + row) % points, 7 * elem] += stiffness[row, 7]
    lam_all = np.zeros((SPEC, s_pad))
    lam_two = (lam[:, None] + lam[None, :]).reshape(-1)
    lam_all[:100, : 10 * elements] = lam_two[:, None] + np.repeat(lam, elements)[None, :]
    segments = np.zeros((coarse_count, z_pad))
    for row in range(coarse_count):
        length = points // coarse_count
        segments[row, row * length : (row + 1) * length] = 1.0
    window_high, window_low = halves(window)
    back_high, back_low = halves(window.T)
    inner = place_a.reshape(10, 10, STACK)[1:9, 1:9].reshape(OWN, STACK)
    single = lambda value: np.asarray(value, np.float32)
    return (
        left_exact(pick_a),
        left_split(spectral_in),
        left_split(spectral_out),
        left_exact(pick_a @ place_s),
        left_split(pick_a @ plane),
        left_exact(inner),
        window_high,
        window_low,
        back_high,
        back_low,
        single(own_cols),
        single(before_cols),
        single(lam_all),
        single(spread),
        single(lines),
        single(segments),
        single((pick_a @ plane_weight)[:, None]),
    )


def split_two(value):
    high = value.astype(jnp.bfloat16)
    return high, (value - high.astype(jnp.float32)).astype(jnp.bfloat16)


def mul(left, right):
    return jnp.dot(left, right, preferred_element_type=jnp.float32)


def left_mul(matrix_ref, value):
    high, low = split_two(value)
    return mul(matrix_ref[...], jnp.concatenate([high, high, low], axis=0))


def left_place(matrix_ref, value):
    high = value.astype(jnp.bfloat16)
    rest = value - high.astype(jnp.float32)
    middle, low = split_two(rest)
    return mul(matrix_ref[...], jnp.concatenate([high, middle, low], axis=0))


def right_mul(value, high_ref, low_ref):
    high, low = split_two(value)
    return mul(high, high_ref[...]) + (mul(high, low_ref[...]) + mul(low, high_ref[...]))


def each_other(count, act):
    if count <= 8:
        for step in range(1, count):
            act(step)
    else:

        def body(step, carry):
            act(step)
            return carry

        lax.fori_loop(1, count, body, 0)


def kernel(
    n_gx, n_gy, rhs, stiff, mass, factor,
    pick_a, spec_in, spec_out, pick_place, plane, inner, win_h, win_l, back_h, back_l,
    own_cols, before_cols, lam_all, spread, lines, segments, plane_weight,
    out_x, out_r,
    stack, sending, coarse_x, coarse_y, sums_x, sums_y, z_high, z_low, scale, first, field_w,
    halo_send, halo_recv, cx_send, cx_recv, cy_send, cy_recv, sx_send, sx_recv, sy_send, sy_recv,
):
    me_x, me_y = lax.axis_index("gx"), lax.axis_index("gy")
    points = rhs.shape[2]
    z_pad = win_h.shape[0]
    s_pad = win_h.shape[1]

    def beside(off_x, off_y):
        return (lax.rem(me_x + off_x + n_gx, n_gx), lax.rem(me_y + off_y + n_gy, n_gy))

    barrier = pltpu.get_barrier_semaphore()

    def greet(where):
        pl.semaphore_signal(barrier, inc=1, device_id=where, device_id_type=MESH)

    each_other(n_gx, lambda step: greet(beside(step, 0)))
    each_other(n_gy, lambda step: greet(beside(0, step)))
    for off_x, off_y, _, _ in SLOTS[4:]:
        greet(beside(off_x, off_y))

    def halo_copy(turn, slot):
        off_x, off_y, start, rows = SLOTS[slot]
        return pltpu.make_async_remote_copy(
            src_ref=sending.at[turn, pl.ds(start, rows)],
            dst_ref=stack.at[turn, pl.ds(start, rows)],
            send_sem=halo_send.at[turn, slot],
            recv_sem=halo_recv.at[turn, slot],
            device_id=beside(-off_x, -off_y),
            device_id_type=MESH,
        )

    def halo_start(turn, rows):
        sending[turn] = rows
        for slot in range(8):
            halo_copy(turn, slot).start()
        stack[turn, pl.ds(0, OWN)] = rows[:OWN]

    def halo_wait(turn):
        for slot in range(8):
            halo_copy(turn, slot).wait_recv()
        return stack[turn]

    def line_copy(buf, send, recv, axis, step, sender):
        return pltpu.make_async_remote_copy(
            src_ref=buf.at[sender],
            dst_ref=buf.at[sender],
            send_sem=send.at[step],
            recv_sem=recv.at[step],
            device_id=beside(step, 0) if axis == 0 else beside(0, step),
            device_id_type=MESH,
        )

    def line_start(buf, send, recv, axis, value):
        me, count = ((me_x, n_gx), (me_y, n_gy))[axis]
        buf[me] = value
        each_other(count, lambda step: line_copy(buf, send, recv, axis, step, me).start())

    def line_total(buf, send, recv, axis):
        me, count = ((me_x, n_gx), (me_y, n_gy))[axis]

        def take(step):
            sender = lax.rem(me - step + count, count)
            line_copy(buf, send, recv, axis, step, sender).wait_recv()

        each_other(count, take)
        return jnp.sum(buf[...], axis=0)

    def line_drain(buf, send, recv, axis):
        me, count = ((me_x, n_gx), (me_y, n_gy))[axis]
        each_other(count, lambda step: line_copy(buf, send, recv, axis, step, me).wait_send())

    cx = [(coarse_x.at[turn], cx_send.at[turn], cx_recv.at[turn], 0) for turn in range(2)]
    cy = [(coarse_y.at[turn], cy_send.at[turn], cy_recv.at[turn], 1) for turn in range(2)]
    sx = (sums_x, sx_send, sx_recv, 0)
    sy = (sums_y, sy_send, sy_recv, 1)

    point = lax.broadcasted_iota(jnp.int32, (OWN, z_pad), 0)
    at_x, at_y = point // 8, point % 8
    coarse_mask = (at_x >= 1) & (at_x <= 6) & (at_y >= 1) & (at_y <= 6)

    def coarse_start(turn, rows):
        line = jnp.sum(jnp.where(coarse_mask, rows, 0.0), axis=0, keepdims=True)
        sums = jnp.sum(segments[...] * line, axis=1, keepdims=True)
        line_start(*cx[turn], jnp.sum(factor[...] * sums, axis=0, keepdims=True))

    def coarse_middle(turn):
        line_start(*cy[turn], line_total(*cx[turn]))

    def coarse_finish(turn):
        total = line_total(*cy[turn])
        values = jnp.sum(factor[...] * total, axis=1, keepdims=True)
        line = jnp.sum(segments[...] * values, axis=0, keepdims=True)
        return jnp.where(coarse_mask, line, 0.0)

    first[...] = jnp.zeros_like(first)
    for row in range(7):
        first[pl.ds(8 * row, 7), pl.ds(0, points)] = rhs[row]
    right = first[...]
    rows = left_place(pick_a, right)
    pl.semaphore_wait(barrier, n_gx - 1 + n_gy - 1 + 4)
    halo_start(0, rows)
    coarse_start(0, right)

    def spread_out(coef):
        flat = jnp.dot(
            jnp.broadcast_to(coef[0], (8, coef.shape[2])), spread[...],
            precision=exact_mode, preferred_element_type=jnp.float32,
        )[0:1]
        return flat[:, :s_pad], flat[:, s_pad : s_pad + z_pad], flat[:, s_pad + z_pad :]

    stiff_s, stiff_own, stiff_before = spread_out(stiff)
    mass_s, mass_own, mass_before = spread_out(mass)
    weight_own, weight_before = lines[0:1, :z_pad], lines[1:2, :z_pad]
    line_stiff = stiff_own * weight_own + stiff_before * weight_before
    line_mass = mass_own * weight_own + mass_before * weight_before
    scale[...] = 1.0 / (stiff_s * lam_all[...] + (mass_s + lines[2:3, :s_pad]))
    diagonal = lax.broadcasted_iota(jnp.int32, (z_pad, z_pad), 0) == lax.broadcasted_iota(
        jnp.int32, (z_pad, z_pad), 1
    )
    along = own_cols[...] * stiff_own + before_cols[...] * stiff_before
    z_high[...], z_low[...] = split_two(along + jnp.where(diagonal, line_mass, 0.0))

    def schwarz(rows):
        spectral = right_mul(left_mul(spec_in, rows), win_h, win_l) * scale[...]
        return left_mul(spec_out, right_mul(spectral, back_h, back_l))

    def element(rows):
        wide = left_place(pick_place, rows)
        field = wide[:OWN]
        result = left_mul(plane, field * line_stiff) + plane_weight[...] * right_mul(
            wide, z_high, z_low
        )
        return field, result

    def precondition(turn, rows):
        coarse_middle(turn)
        result = schwarz(halo_wait(2 * turn))
        halo_start(2 * turn + 1, result)
        plate = coarse_finish(turn)
        stack[2 * turn + 1, pl.ds(0, OWN)] = result[:OWN] + plate

    def dot_line(left, other):
        return jnp.sum(left * other, axis=0, keepdims=True)

    owned = (at_x < 7) & (at_y < 7)

    precondition(0, rows)
    z_field, w_rows = element(halo_wait(1))
    halo_start(2, w_rows)
    w_local = w_rows[:OWN]
    coarse_start(1, w_local)
    precondition(1, w_rows)
    field_w[...] = left_place(inner, stack[2])
    v_field, av_rows = element(halo_wait(3))
    halo_start(4, av_rows)
    av_local = av_rows[:OWN]
    partial = jnp.concatenate(
        [
            dot_line(right, jnp.where(owned, z_field, 0.0)),
            dot_line(z_field, w_local),
            dot_line(right, jnp.where(owned, v_field, 0.0)),
            dot_line(v_field, w_local),
            dot_line(v_field, av_local),
            dot_line(z_field, av_local),
            jnp.zeros((2, z_pad), jnp.float32),
        ],
        axis=0,
    )
    line_start(*sx, partial)
    line_start(*sy, line_total(*sx))
    av_field = left_place(inner, halo_wait(4))
    w_field = field_w[...]
    totals = jnp.sum(line_total(*sy), axis=1, keepdims=True)
    rz, zw, rv, vw, vav, zav = [totals[row : row + 1] for row in range(6)]
    step_0 = rz / zw
    rho_1 = rz - step_0 * (rv + zw) + step_0 * step_0 * vw
    momentum = rho_1 / rz
    curve = (
        zw - step_0 * (vw + zav) + step_0 * step_0 * vav
        + momentum * ((zw - step_0 * vw) + (zw - step_0 * zav))
        + momentum * momentum * zw
    )
    step_1 = rho_1 / curve
    next_dir = (z_field - step_0 * v_field) + momentum * z_field
    next_image = (w_field - step_0 * av_field) + momentum * w_field
    final_x = step_0 * z_field + step_1 * next_dir
    final_r = (right - step_0 * w_field) - step_1 * next_image
    for row in range(7):
        out_x[row] = final_x[8 * row : 8 * row + 7, :points]
        out_r[row] = final_r[8 * row : 8 * row + 7, :points]

    for turn in range(ROUNDS):
        for slot in range(8):
            halo_copy(turn, slot).wait_send()
    for group in (*cx, *cy, sx, sy):
        line_drain(*group)


def local(n_gx, n_gy, right_side, stiff_coef, mass_coef, coarse_factor):
    elements = stiff_coef.shape[2]
    coarse_count, coarse_all = coarse_factor.shape
    tables = constants(elements, coarse_count)
    z_pad = round_up(7 * elements, 128)
    s_pad = round_up(10 * elements, 128)
    dma = pltpu.SemaphoreType.DMA
    single = jnp.float32
    whole = pl.BlockSpec(memory_space=pltpu.VMEM)
    shape = jax.ShapeDtypeStruct(right_side.shape, single)
    return pl.pallas_call(
        functools.partial(kernel, n_gx, n_gy),
        out_shape=(shape, shape),
        in_specs=[whole] * (4 + len(tables)),
        out_specs=(whole, whole),
        scratch_shapes=[
            pltpu.VMEM((ROUNDS, STACK, z_pad), single),
            pltpu.VMEM((ROUNDS, STACK, z_pad), single),
            pltpu.VMEM((2, n_gx, 1, coarse_all), single),
            pltpu.VMEM((2, n_gy, 1, coarse_all), single),
            pltpu.VMEM((n_gx, 8, z_pad), single),
            pltpu.VMEM((n_gy, 8, z_pad), single),
            pltpu.VMEM((z_pad, z_pad), jnp.bfloat16),
            pltpu.VMEM((z_pad, z_pad), jnp.bfloat16),
            pltpu.VMEM((SPEC, s_pad), single),
            pltpu.VMEM((OWN, z_pad), single),
            pltpu.VMEM((OWN, z_pad), single),
            dma((ROUNDS, 8)),
            dma((ROUNDS, 8)),
            dma((2, n_gx)),
            dma((2, n_gx)),
            dma((2, n_gy)),
            dma((2, n_gy)),
            dma((n_gx,)),
            dma((n_gx,)),
            dma((n_gy,)),
            dma((n_gy,)),
        ],
        compiler_params=pltpu.CompilerParams(
            collective_id=0, has_side_effects=True, vmem_limit_bytes=40 * 1024 * 1024
        ),
    )(right_side, stiff_coef, mass_coef, coarse_factor, *[jnp.asarray(table) for table in tables])


def solution(mesh):
    placed = (P("gx", "gy", None), P("gx", "gy", None), P("gx", "gy", None), P(("gx", "gy"), None))
    return jax.shard_map(
        functools.partial(local, mesh.shape["gx"], mesh.shape["gy"]),
        mesh=mesh,
        in_specs=placed,
        out_specs=(P("gx", "gy", None), P("gx", "gy", None)),
        check_vma=False,
    )
```

time: 206 us -> 53 us (0.26)
  blocking collectives: 78 us -> 0 us
  starting transfers between devices: 50.9 us -> 0 us
  Pallas kernels: 0 us -> 33.4 us
  waiting for transfers between devices: 24.3 us -> 0 us
  matrix products: 16 us -> 0 us
  other arithmetic: 9.91 us -> 0 us
  between operations: 7.53 us -> 0.68 us
    psum x2 -> x0, blocking collectives: 78 us -> none  [global_pair(): lax.psum((jnp.sum(owned_part(current) * smooth[:7, :7]), jnp.sum(smooth[:...]
    ppermute x30 -> x0, starting transfers between devices: 50.9 us -> none  [the longest x10 24.3 us: with_halo(): lax.ppermute(lax.slice_in_dim(block, 0, width, axis=dim), axis, backward)]
    pallas_call x0 -> x1, Pallas kernels: none -> 33.4 us  [local(): pl.pallas_call(functools.partial(kernel, n_gx, n_gy), out_shape=(shape, s...]
    ppermute x30 -> x0, waiting for transfers between devices: 24.3 us -> none  [the longest x10 9.82 us: swapped(): lax.ppermute(shard, axis, [(i, i ^ 1 << apart) for i in range(lax.axis_si...]
    unnamed x31 -> x44, local copies, waits for them, and re-layouts: 0.21 us -> 18.3 us
    dot_general x22 -> x0, matrix products: 16 us -> none  [the longest x2 2.4 us: local_solve(): jnp.einsum('bj,ajte->abte', eigen_basis, restored, precision=exact_mode)]
    slice x58 -> x0, local copies, waits for them, and re-layouts: 5.1 us -> none  [the longest x13 2.05 us: with_halo(): lax.slice_in_dim(block, block.shape[dim] - width, None, axis=dim)]
    reshape x14 -> x0, local copies, waits for them, and re-layouts: 4.84 us -> none  [the longest x6 3.21 us: z_windows(): blocks = jnp.moveaxis(field_in.reshape(leading + (elements, 7)), 2, 3)]
  transfers between devices with their start and end apart: 30 -> 0, of which waited for: 19 -> 0; matrix products, arithmetic and copies ran while one was open for 6% -> 0% of each run, Pallas kernels for 0% -> 0%
where the time goes in v1:
time: 53 us; the launch traced here: 52.3 us
  Pallas kernels  33.4 us (63%)
  local copies, waits for them, and re-layouts  18.3 us (35%)
  between operations  0.68 us (1%)
    pallas_call x1, Pallas kernels, local(): pl.pallas_call(functools.partial(kernel, n_gx, n_gy), out_shape=(shape, s...  33.4 us
    unnamed x44, local copies, waits for them, and re-layouts  18.3 us

profile of v1, /device:TPU:0, one launch (start us, length us, event | category | flops | bytes accessed | tf_op | source)
XLA Modules:
  0.0 52.3 jit_solution(13269154037672490760)
XLA Ops:
  0.6 0.0 copy-start.18
  0.6 0.0 copy-start.17
  0.7 0.7 %copy-done.18 = f32[8,256]{1,0:T(8,128)S(1)} copy-done((f32[8,256]{1,0:T(8,128)S(1)}, f32[8,256]{1,0:T(8,128)}, u32[]{:S(2)}) %copy-start.18) | copy-done | bytes 8216
  1.3 0.0 copy-done.17
  1.3 0.0 copy-start
  1.3 0.9 %copy-done = f32[256,256]{1,0:T(8,128)S(1)} copy-done((f32[256,256]{1,0:T(8,128)S(1)}, f32[256,256]{1,0:T(8,128)}, u32[]{:S(2)}) %copy-start) | copy-done | bytes 262168
  2.3 0.0 copy-start.1
  2.3 0.9 %copy-done.1 = f32[256,256]{1,0:T(8,128)S(1)} copy-done((f32[256,256]{1,0:T(8,128)S(1)}, f32[256,256]{1,0:T(8,128)}, u32[]{:S(2)}) %copy-start.1) | copy-done | bytes 262168
  3.2 0.0 copy-start.2
  3.3 0.9 %copy-done.2 = bf16[160,480]{1,0:T(8,128)(2,1)S(1)} copy-done((bf16[160,480]{1,0:T(8,128)(2,1)S(1)}, bf16[160,480]{1,0:T(8,128)(2,1)}, u32[]{:S(2)}) %copy-start.2) | copy-done | bytes 153624
  4.2 0.0 copy-start.3
  4.2 0.9 %copy-done.3 = bf16[256,256]{1,0:T(8,128)(2,1)S(1)} copy-done((bf16[256,256]{1,0:T(8,128)(2,1)S(1)}, bf16[256,256]{1,0:T(8,128)(2,1)}, u32[]{:S(2)}) %copy-start.3) | copy-done | bytes 131096
  5.1 0.9 %copy-done.4 = bf16[256,256]{1,0:T(8,128)(2,1)S(1)} copy-done((bf16[256,256]{1,0:T(8,128)(2,1)S(1)}, bf16[256,256]{1,0:T(8,128)(2,1)}, u32[]{:S(2)}) %copy-start.4) | copy-done | bytes 131096
  6.0 0.0 copy-start.5
  6.0 0.9 %copy-done.5 = bf16[256,256]{1,0:T(8,128)(2,1)S(1)} copy-done((bf16[256,256]{1,0:T(8,128)(2,1)S(1)}, bf16[256,256]{1,0:T(8,128)(2,1)}, u32[]{:S(2)}) %copy-start.5) | copy-done | bytes 131096
  6.9 0.0 copy-start.6
  6.9 0.9 %copy-done.6 = bf16[256,256]{1,0:T(8,128)(2,1)S(1)} copy-done((bf16[256,256]{1,0:T(8,128)(2,1)S(1)}, bf16[256,256]{1,0:T(8,128)(2,1)}, u32[]{:S(2)}) %copy-start.6) | copy-done | bytes 131096
  7.8 0.9 %copy-done.7 = bf16[160,336]{1,0:T(8,128)(2,1)S(1)} copy-done((bf16[160,336]{1,0:T(8,128)(2,1)S(1)}, bf16[160,336]{1,0:T(8,128)(2,1)}, u32[]{:S(2)}) %copy-start.7) | copy-done | bytes 107544
  8.7 0.9 %copy-done.8 = f32[112,256]{1,0:T(8,128)S(1)} copy-done((f32[112,256]{1,0:T(8,128)S(1)}, f32[112,256]{1,0:T(8,128)}, u32[]{:S(2)}) %copy-start.8) | copy-done | bytes 114712
  9.6 0.9 %copy-done.9 = bf16[112,480]{1,0:T(8,128)(2,1)S(1)} copy-done((bf16[112,480]{1,0:T(8,128)(2,1)S(1)}, bf16[112,480]{1,0:T(8,128)(2,1)}, u32[]{:S(2)}) %copy-start.9) | copy-done | bytes 107544
  10.5 0.9 %copy-done.10 = f32[160,1]{1,0:T(8,128)S(1)} copy-done((f32[160,1]{1,0:T(8,128)S(1)}, f32[160,1]{1,0:T(8,128)}, u32[]{:S(2)}) %copy-start.10) | copy-done | bytes 664
  11.4 0.9 %copy-done.11 = bf16[160,192]{1,0:T(8,128)(2,1)S(1)} copy-done((bf16[160,192]{1,0:T(8,128)(2,1)S(1)}, bf16[160,192]{1,0:T(8,128)(2,1)}, u32[]{:S(2)}) %copy-start.11) | copy-done | bytes 61464
  12.3 0.9 %copy-done.12 = bf16[160,192]{1,0:T(8,128)(2,1)S(1)} copy-done((bf16[160,192]{1,0:T(8,128)(2,1)S(1)}, bf16[160,192]{1,0:T(8,128)(2,1)}, u32[]{:S(2)}) %copy-start.12) | copy-done | bytes 61464
  13.1 0.9 %copy-done.13 = f32[24,768]{1,0:T(8,128)S(1)} copy-done((f32[24,768]{1,0:T(8,128)S(1)}, f32[24,768]{1,0:T(8,128)}, u32[]{:S(2)}) %copy-start.13) | copy-done | bytes 73752
  14.0 0.8 %copy-done.14 = bf16[64,480]{1,0:T(8,128)(2,1)S(1)} copy-done((bf16[64,480]{1,0:T(8,128)(2,1)S(1)}, bf16[64,480]{1,0:T(8,128)(2,1)}, u32[]{:S(2)}) %copy-start.14) | copy-done | bytes 61464
  14.9 0.8 %copy-done.15 = f32[7,7,168]{2,1,0:T(8,128)S(1)} copy-done((f32[7,7,168]{2,1,0:T(8,128)S(1)}, f32[7,7,168]{2,1,0:T(8,128)}, u32[]{:S(2)}) %copy-start.15) | copy-done | bytes 32952
  15.7 0.7 %copy-done.16 = f32[8,256]{1,0:T(8,128)S(1)} copy-done((f32[8,256]{1,0:T(8,128)S(1)}, f32[8,256]{1,0:T(8,128)}, u32[]{:S(2)}) %copy-start.16) | copy-done | bytes 8216
  16.4 0.7 %copy-done.19 = f32[1,1,24]{2,1,0:T(1,128)S(1)} copy-done((f32[1,1,24]{2,1,0:T(1,128)S(1)}, f32[1,1,24]{2,1,0:T(1,128)}, u32[]{:S(2)}) %copy-start.19) | copy-done | bytes 120
  17.0 0.7 %copy-done.20 = f32[1,1,24]{2,1,0:T(1,128)S(1)} copy-done((f32[1,1,24]{2,1,0:T(1,128)S(1)}, f32[1,1,24]{2,1,0:T(1,128)}, u32[]{:S(2)}) %copy-start.20) | copy-done | bytes 120
  17.7 33.4 %shard_map.212 = (f32[7,7,168]{2,1,0:T(8,128)S(1)}, f32[7,7,168]{2,1,0:T(8,128)S(1)}) custom-call(f32[7,7,168]{2,1,0:T(8,128)S(1)} %copy-done.15, f32[1,1,24]{2,1,0:T(1,128)S(1)} %copy-done.19, f32[1,1,24]{2,1,0:T(1,128)S(1)} %copy-done.20, f32[8,256]{1,0:T(8,128)S(1)} %copy-done.16, bf16[160,192]{1,0:T(8,128)(2,1)S(1)} %copy-done.12, ...), custom_call_target="tpu_custom_call" | custom-call | tf_op jit(solution)/shard_map/pallas_call | solution.py:475
  51.1 0.6 %copy.25 = f32[7,7,168]{2,1,0:T(8,128)} copy(f32[7,7,168]{2,1,0:T(8,128)S(1)} %get-tuple-element.4) | data formatting | bytes 65856
  51.7 0.6 %copy.26 = f32[7,7,168]{2,1,0:T(8,128)} copy(f32[7,7,168]{2,1,0:T(8,128)S(1)} %get-tuple-element.5) | data formatting | bytes 65856
  (13 shorter events, 0.0 us)
Async XLA Ops:
  0.6 0.7 %copy-start.18 = (f32[8,256]{1,0:T(8,128)S(1)}, f32[8,256]{1,0:T(8,128)}, u32[]{:S(2)}) copy-start(f32[8,256]{1,0:T(8,128)} %constant.48.clone.lines) | copy-start | bytes 24580
  0.6 0.7 %copy-start.17 = (f32[8,256]{1,0:T(8,128)S(1)}, f32[8,256]{1,0:T(8,128)}, u32[]{:S(2)}) copy-start(f32[8,256]{1,0:T(8,128)} %constant.49.clone.segments) | copy-start | bytes 24580
  1.3 0.9 %copy-start = (f32[256,256]{1,0:T(8,128)S(1)}, f32[256,256]{1,0:T(8,128)}, u32[]{:S(2)}) copy-start(f32[256,256]{1,0:T(8,128)} %constant.45.clone.before_cols) | copy-start | bytes 786436
  2.3 0.9 %copy-start.1 = (f32[256,256]{1,0:T(8,128)S(1)}, f32[256,256]{1,0:T(8,128)}, u32[]{:S(2)}) copy-start(f32[256,256]{1,0:T(8,128)} %constant.44.clone.own_cols) | copy-start | bytes 786436
  3.2 0.9 %copy-start.2 = (bf16[160,480]{1,0:T(8,128)(2,1)S(1)}, bf16[160,480]{1,0:T(8,128)(2,1)}, u32[]{:S(2)}) copy-start(bf16[160,480]{1,0:T(8,128)(2,1)} %constant.37.clone.pick_place) | copy-start | bytes 460804
  4.2 0.9 %copy-start.3 = (bf16[256,256]{1,0:T(8,128)(2,1)S(1)}, bf16[256,256]{1,0:T(8,128)(2,1)}, u32[]{:S(2)}) copy-start(bf16[256,256]{1,0:T(8,128)(2,1)} %constant.43.clone.back_l) | copy-start | bytes 393220
  5.1 0.9 %copy-start.4 = (bf16[256,256]{1,0:T(8,128)(2,1)S(1)}, bf16[256,256]{1,0:T(8,128)(2,1)}, u32[]{:S(2)}) copy-start(bf16[256,256]{1,0:T(8,128)(2,1)} %constant.42.clone.back_h) | copy-start | bytes 393220
  6.0 0.9 %copy-start.5 = (bf16[256,256]{1,0:T(8,128)(2,1)S(1)}, bf16[256,256]{1,0:T(8,128)(2,1)}, u32[]{:S(2)}) copy-start(bf16[256,256]{1,0:T(8,128)(2,1)} %constant.41.clone.win_l) | copy-start | bytes 393220
  6.9 0.9 %copy-start.6 = (bf16[256,256]{1,0:T(8,128)(2,1)S(1)}, bf16[256,256]{1,0:T(8,128)(2,1)}, u32[]{:S(2)}) copy-start(bf16[256,256]{1,0:T(8,128)(2,1)} %constant.40.clone.win_h) | copy-start | bytes 393220
  7.8 0.9 %copy-start.7 = (bf16[160,336]{1,0:T(8,128)(2,1)S(1)}, bf16[160,336]{1,0:T(8,128)(2,1)}, u32[]{:S(2)}) copy-start(bf16[160,336]{1,0:T(8,128)(2,1)} %constant.36.clone.spec_out) | copy-start | bytes 322564
  8.7 0.9 %copy-start.8 = (f32[112,256]{1,0:T(8,128)S(1)}, f32[112,256]{1,0:T(8,128)}, u32[]{:S(2)}) copy-start(f32[112,256]{1,0:T(8,128)} %constant.46.clone.lam_all) | copy-start | bytes 344068
  9.6 0.9 %copy-start.9 = (bf16[112,480]{1,0:T(8,128)(2,1)S(1)}, bf16[112,480]{1,0:T(8,128)(2,1)}, u32[]{:S(2)}) copy-start(bf16[112,480]{1,0:T(8,128)(2,1)} %constant.35.clone.spec_in) | copy-start | bytes 322564
  10.5 0.9 %copy-start.10 = (f32[160,1]{1,0:T(8,128)S(1)}, f32[160,1]{1,0:T(8,128)}, u32[]{:S(2)}) copy-start(f32[160,1]{1,0:T(8,128)} %constant.50.clone.plane_weight) | copy-start | bytes 1924
  11.4 0.9 %copy-start.11 = (bf16[160,192]{1,0:T(8,128)(2,1)S(1)}, bf16[160,192]{1,0:T(8,128)(2,1)}, u32[]{:S(2)}) copy-start(bf16[160,192]{1,0:T(8,128)(2,1)} %constant.38.clone.plane) | copy-start | bytes 184324
  12.3 0.9 %copy-start.12 = (bf16[160,192]{1,0:T(8,128)(2,1)S(1)}, bf16[160,192]{1,0:T(8,128)(2,1)}, u32[]{:S(2)}) copy-start(bf16[160,192]{1,0:T(8,128)(2,1)} %constant.34.clone.pick_a) | copy-start | bytes 184324
  13.1 0.9 %copy-start.13 = (f32[24,768]{1,0:T(8,128)S(1)}, f32[24,768]{1,0:T(8,128)}, u32[]{:S(2)}) copy-start(f32[24,768]{1,0:T(8,128)} %constant.47.clone.spread) | copy-start | bytes 221188
  14.0 0.8 %copy-start.14 = (bf16[64,480]{1,0:T(8,128)(2,1)S(1)}, bf16[64,480]{1,0:T(8,128)(2,1)}, u32[]{:S(2)}) copy-start(bf16[64,480]{1,0:T(8,128)(2,1)} %constant.39.clone.inner) | copy-start | bytes 184324
  14.9 0.8 %copy-start.15 = (f32[7,7,168]{2,1,0:T(8,128)S(1)}, f32[7,7,168]{2,1,0:T(8,128)}, u32[]{:S(2)}) copy-start(f32[7,7,168]{2,1,0:T(8,128)} %rhs.1) | copy-start | bytes 98788
  15.7 0.7 %copy-start.16 = (f32[8,256]{1,0:T(8,128)S(1)}, f32[8,256]{1,0:T(8,128)}, u32[]{:S(2)}) copy-start(f32[8,256]{1,0:T(8,128)} %factor.1) | copy-start | bytes 24580
  16.4 0.7 %copy-start.19 = (f32[1,1,24]{2,1,0:T(1,128)S(1)}, f32[1,1,24]{2,1,0:T(1,128)}, u32[]{:S(2)}) copy-start(f32[1,1,24]{2,1,0:T(1,128)} %stiff.1) | copy-start | bytes 292
  17.0 0.7 %copy-start.20 = (f32[1,1,24]{2,1,0:T(1,128)S(1)}, f32[1,1,24]{2,1,0:T(1,128)}, u32[]{:S(2)}) copy-start(f32[1,1,24]{2,1,0:T(1,128)} %mass.1) | copy-start | bytes 292

commit v2 on v1

--- a/solution.py
+++ b/solution.py
@@ -26,6 +26,12 @@
 )
 STACK = 160
 SPEC = 112
+LAST = ((72, 0), (104, 2), (128, 4))
+OPERANDS = (
+    "rhs", "pick_a", "segments", "factor", "stiff", "mass", "spread", "lines", "lam_all", "own_cols", "before_cols",
+    "spec_in", "win_h", "win_l", "back_h", "back_l", "spec_out", "pick_place", "plane", "plane_weight", "inner",
+)
+DIRECT = 64
 
 
 def legendre_pair(position, degree):
@@ -119,11 +125,15 @@
     place = np.zeros((size_to * size_to, STACK))
     for off_x, off_y, start, _ in ((0, 0, 0, OWN),) + SLOTS:
         row = start
-        for from_x, to_x in zip(taken[off_x], placed[off_x]):
-            for from_y, to_y in zip(taken[off_y], placed[off_y]):
-                pick[row, from_x * size_from + from_y] = 1.0
-                place[to_x * size_to + to_y, row] = 1.0
-                row += 1
+        pairs_x = list(zip(taken[off_x], placed[off_x]))
+        pairs_y = list(zip(taken[off_y], placed[off_y]))
+        pairs = [(one, two) for one in pairs_x for two in pairs_y]
+        if off_x == 0 and off_y != 0:
+            pairs = [(one, two) for two in pairs_y for one in pairs_x]
+        for (from_x, to_x), (from_y, to_y) in pairs:
+            pick[row, from_x * size_from + from_y] = 1.0
+            place[to_x * size_to + to_y, row] = 1.0
+            row += 1
     return pick, place
 
 
@@ -197,26 +207,27 @@
     window_high, window_low = halves(window)
     back_high, back_low = halves(window.T)
     inner = place_a.reshape(10, 10, STACK)[1:9, 1:9].reshape(OWN, STACK)
+    inner = np.concatenate([inner[:, start : start + 8] for start, _ in LAST] + [np.zeros((OWN, 8))], axis=1)
     single = lambda value: np.asarray(value, np.float32)
-    return (
-        left_exact(pick_a),
-        left_split(spectral_in),
-        left_split(spectral_out),
-        left_exact(pick_a @ place_s),
-        left_split(pick_a @ plane),
-        left_exact(inner),
-        window_high,
-        window_low,
-        back_high,
-        back_low,
-        single(own_cols),
-        single(before_cols),
-        single(lam_all),
-        single(spread),
-        single(lines),
-        single(segments),
-        single((pick_a @ plane_weight)[:, None]),
-    )
+    return {
+        "pick_a": left_exact(pick_a),
+        "spec_in": left_split(spectral_in),
+        "spec_out": left_split(spectral_out),
+        "pick_place": left_exact(pick_a @ place_s),
+        "plane": left_split(pick_a @ plane),
+        "inner": left_exact(inner),
+        "win_h": window_high,
+        "win_l": window_low,
+        "back_h": back_high,
+        "back_l": back_low,
+        "own_cols": single(own_cols),
+        "before_cols": single(before_cols),
+        "lam_all": single(lam_all),
+        "spread": single(spread),
+        "lines": single(lines),
+        "segments": single(segments),
+        "plane_weight": single((pick_a @ plane_weight)[:, None]),
+    }
 
 
 def split_two(value):
@@ -258,34 +269,69 @@
         lax.fori_loop(1, count, body, 0)
 
 
-def kernel(
-    n_gx, n_gy, rhs, stiff, mass, factor,
-    pick_a, spec_in, spec_out, pick_place, plane, inner, win_h, win_l, back_h, back_l,
-    own_cols, before_cols, lam_all, spread, lines, segments, plane_weight,
-    out_x, out_r,
-    stack, sending, coarse_x, coarse_y, sums_x, sums_y, z_high, z_low, scale, first, field_w,
-    halo_send, halo_recv, cx_send, cx_recv, cy_send, cy_recv, sx_send, sx_recv, sy_send, sy_recv,
-):
+def stages_of(n_gx, n_gy):
+    return ("xy",) if n_gx * n_gy <= DIRECT else ("x", "y")
+
+
+def stage_size(stage, n_gx, n_gy):
+    return {"x": n_gx, "y": n_gy, "xy": n_gx * n_gy}[stage]
+
+
+def kernel(n_gx, n_gy, n_in, *refs):
+    sources = refs[:n_in]
+    out_x, out_r = refs[n_in : n_in + 2]
+    loaded = refs[n_in + 2 : 2 * n_in + 2]
+    load_sem, stack, sending, z_high, z_low, scale, first, field_w, halo_send, halo_recv = refs[
+        2 * n_in + 2 : 2 * n_in + 12
+    ]
+    lanes = refs[2 * n_in + 12 :]
+    (
+        rhs, pick_a, segments, factor, stiff, mass, spread, lines, lam_all, own_cols, before_cols,
+        spec_in, win_h, win_l, back_h, back_l, spec_out, pick_place, plane, plane_weight, inner,
+    ) = loaded
+    loads = [
+        pltpu.make_async_copy(source, target, load_sem.at[index])
+        for index, (source, target) in enumerate(zip(sources, loaded))
+    ]
+    for load in loads:
+        load.start()
+
     me_x, me_y = lax.axis_index("gx"), lax.axis_index("gy")
     points = rhs.shape[2]
     z_pad = win_h.shape[0]
     s_pad = win_h.shape[1]
+    stages = stages_of(n_gx, n_gy)
 
     def beside(off_x, off_y):
         return (lax.rem(me_x + off_x + n_gx, n_gx), lax.rem(me_y + off_y + n_gy, n_gy))
 
+    def each_offset(stage, act):
+        if stage == "xy":
+            for off_x in range(n_gx):
+                for off_y in range(n_gy):
+                    if off_x or off_y:
+                        act(off_x, off_y)
+        elif stage == "x":
+            each_other(n_gx, lambda step: act(step, 0))
+        else:
+            each_other(n_gy, lambda step: act(0, step))
+
     barrier = pltpu.get_barrier_semaphore()
 
-    def greet(where):
-        pl.semaphore_signal(barrier, inc=1, device_id=where, device_id_type=MESH)
-
-    each_other(n_gx, lambda step: greet(beside(step, 0)))
-    each_other(n_gy, lambda step: greet(beside(0, step)))
-    for off_x, off_y, _, _ in SLOTS[4:]:
-        greet(beside(off_x, off_y))
-
-    def halo_copy(turn, slot):
-        off_x, off_y, start, rows = SLOTS[slot]
+    def greet(off_x, off_y):
+        pl.semaphore_signal(barrier, inc=1, device_id=beside(off_x, off_y), device_id_type=MESH)
+
+    greeted = 0
+    for stage in stages:
+        each_offset(stage, greet)
+        greeted += stage_size(stage, n_gx, n_gy) - 1
+    if stages != ("xy",):
+        for off_x, off_y, _, _ in SLOTS[4:]:
+            greet(off_x, off_y)
+        greeted += 4
+
+    def halo_copy(turn, slot, start, rows):
+        off_x, off_y, _, _ = SLOTS[slot]
         return pltpu.make_async_remote_copy(
             src_ref=sending.at[turn, pl.ds(start, rows)],
             dst_ref=stack.at[turn, pl.ds(start, rows)],
@@ -295,50 +341,67 @@
             device_id_type=MESH,
         )
 
+    def halo_copies(turn):
+        if turn == ROUNDS - 1:
+            return [halo_copy(turn, slot, start, 8) for start, slot in LAST]
+        return [halo_copy(turn, slot, SLOTS[slot][2], SLOTS[slot][3]) for slot in range(8)]
+
     def halo_start(turn, rows):
         sending[turn] = rows
-        for slot in range(8):
-            halo_copy(turn, slot).start()
+        for copy in halo_copies(turn):
+            copy.start()
         stack[turn, pl.ds(0, OWN)] = rows[:OWN]
 
     def halo_wait(turn):
-        for slot in range(8):
-            halo_copy(turn, slot).wait_recv()
-        return stack[turn]
-
-    def line_copy(buf, send, recv, axis, step, sender):
-        return pltpu.make_async_remote_copy(
-            src_ref=buf.at[sender],
-            dst_ref=buf.at[sender],
-            send_sem=send.at[step],
-            recv_sem=recv.at[step],
-            device_id=beside(step, 0) if axis == 0 else beside(0, step),
-            device_id_type=MESH,
-        )
-
-    def line_start(buf, send, recv, axis, value):
-        me, count = ((me_x, n_gx), (me_y, n_gy))[axis]
-        buf[me] = value
-        each_other(count, lambda step: line_copy(buf, send, recv, axis, step, me).start())
-
-    def line_total(buf, send, recv, axis):
-        me, count = ((me_x, n_gx), (me_y, n_gy))[axis]
-
-        def take(step):
-            sender = lax.rem(me - step + count, count)
-            line_copy(buf, send, recv, axis, step, sender).wait_recv()
-
-        each_other(count, take)
-        return jnp.sum(buf[...], axis=0)
-
-    def line_drain(buf, send, recv, axis):
-        me, count = ((me_x, n_gx), (me_y, n_gy))[axis]
-        each_other(count, lambda step: line_copy(buf, send, recv, axis, step, me).wait_send())
-
-    cx = [(coarse_x.at[turn], cx_send.at[turn], cx_recv.at[turn], 0) for turn in range(2)]
-    cy = [(coarse_y.at[turn], cy_send.at[turn], cy_recv.at[turn], 1) for turn in range(2)]
-    sx = (sums_x, sx_send, sx_recv, 0)
-    sy = (sums_y, sy_send, sy_recv, 1)
+        for copy in halo_copies(turn):
+            copy.wait_recv()
+
+    def slot_of(stage, off_x, off_y):
+        at_x, at_y = beside(off_x, off_y)
+        return {"x": at_x, "y": at_y, "xy": at_x * n_gy + at_y}[stage]
+
+    class Lane:
+        def __init__(self, buffers):
+            self.legs = [(stage,) + tuple(buffers[3 * at : 3 * at + 3]) for at, stage in enumerate(stages)]
+
+        def copy(self, leg, off_x, off_y, slot):
+            _, buf, send, recv = leg
+            return pltpu.make_async_remote_copy(
+                src_ref=buf.at[slot],
+                dst_ref=buf.at[slot],
+                send_sem=send.at[off_x * n_gy + off_y if leg[0] == "xy" else off_x + off_y],
+                recv_sem=recv.at[off_x * n_gy + off_y if leg[0] == "xy" else off_x + off_y],
+                device_id=beside(off_x, off_y),
+                device_id_type=MESH,
+            )
+
+        def put(self, leg, value):
+            mine = slot_of(leg[0], 0, 0)
+            leg[1][mine] = value
+            each_offset(leg[0], lambda x, y: self.copy(leg, x, y, mine).start())
+
+        def take(self, leg):
+            each_offset(leg[0], lambda x, y: self.copy(leg, x, y, slot_of(leg[0], -x, -y)).wait_recv())
+            return jnp.sum(leg[1][...], axis=0)
+
+        def start(self, value):
+            self.put(self.legs[0], value)
+
+        def middle(self):
+            for before, after in zip(self.legs, self.legs[1:]):
+                self.put(after, self.take(before))
+
+        def finish(self):
+            return self.take(self.legs[-1])
+
+        def drain(self):
+            for leg in self.legs:
+                mine = slot_of(leg[0], 0, 0)
+                each_offset(leg[0], lambda x, y: self.copy(leg, x, y, mine).wait_send())
+
+    per_lane = 3 * len(stages)
+    coarse = [Lane(lanes[:per_lane]), Lane(lanes[per_lane : 2 * per_lane])]
+    sums = Lane(lanes[2 * per_lane :])
 
     point = lax.broadcasted_iota(jnp.int32, (OWN, z_pad), 0)
     at_x, at_y = point // 8, point % 8
@@ -346,26 +409,28 @@
 
     def coarse_start(turn, rows):
         line = jnp.sum(jnp.where(coarse_mask, rows, 0.0), axis=0, keepdims=True)
-        sums = jnp.sum(segments[...] * line, axis=1, keepdims=True)
-        line_start(*cx[turn], jnp.sum(factor[...] * sums, axis=0, keepdims=True))
-
-    def coarse_middle(turn):
-        line_start(*cy[turn], line_total(*cx[turn]))
+        held = jnp.sum(segments[...] * line, axis=1, keepdims=True)
+        coarse[turn].start(jnp.sum(factor[...] * held, axis=0, keepdims=True))
 
     def coarse_finish(turn):
-        total = line_total(*cy[turn])
+        total = coarse[turn].finish()
         values = jnp.sum(factor[...] * total, axis=1, keepdims=True)
         line = jnp.sum(segments[...] * values, axis=0, keepdims=True)
         return jnp.where(coarse_mask, line, 0.0)
 
     first[...] = jnp.zeros_like(first)
+    for load in loads[:4]:
+        load.wait()
     for row in range(7):
         first[pl.ds(8 * row, 7), pl.ds(0, points)] = rhs[row]
     right = first[...]
     rows = left_place(pick_a, right)
-    pl.semaphore_wait(barrier, n_gx - 1 + n_gy - 1 + 4)
+    pl.semaphore_wait(barrier, greeted)
     halo_start(0, rows)
     coarse_start(0, right)
+
+    for load in loads[4:11]:
+        load.wait()
 
     def spread_out(coef):
         flat = jnp.dot(
@@ -386,6 +451,9 @@
     along = own_cols[...] * stiff_own + before_cols[...] * stiff_before
     z_high[...], z_low[...] = split_two(along + jnp.where(diagonal, line_mass, 0.0))
 
+    for load in loads[11:]:
+        load.wait()
+
     def schwarz(rows):
         spectral = right_mul(left_mul(spec_in, rows), win_h, win_l) * scale[...]
         return left_mul(spec_out, right_mul(spectral, back_h, back_l))
@@ -398,9 +466,10 @@
         )
         return field, result
 
-    def precondition(turn, rows):
-        coarse_middle(turn)
-        result = schwarz(halo_wait(2 * turn))
+    def precondition(turn):
+        coarse[turn].middle()
+        halo_wait(2 * turn)
+        result = schwarz(stack[2 * turn])
         halo_start(2 * turn + 1, result)
         plate = coarse_finish(turn)
         stack[2 * turn + 1, pl.ds(0, OWN)] = result[:OWN] + plate
@@ -408,16 +477,22 @@
     def dot_line(left, other):
         return jnp.sum(left * other, axis=0, keepdims=True)
 
+    def gathered(turn, own):
+        parts = [stack[turn, pl.ds(start, 8)] for start, _ in LAST]
+        return own + left_place(inner, jnp.concatenate(parts + [jnp.zeros_like(parts[0])], axis=0))
+
     owned = (at_x < 7) & (at_y < 7)
 
-    precondition(0, rows)
-    z_field, w_rows = element(halo_wait(1))
+    precondition(0)
+    halo_wait(1)
+    z_field, w_rows = element(stack[1])
     halo_start(2, w_rows)
     w_local = w_rows[:OWN]
     coarse_start(1, w_local)
-    precondition(1, w_rows)
-    field_w[...] = left_place(inner, stack[2])
-    v_field, av_rows = element(halo_wait(3))
+    precondition(1)
+    field_w[...] = gathered(2, w_local)
+    halo_wait(3)
+    v_field, av_rows = element(stack[3])
     halo_start(4, av_rows)
     av_local = av_rows[:OWN]
     partial = jnp.concatenate(
@@ -432,12 +507,16 @@
         ],
         axis=0,
     )
-    line_start(*sx, partial)
-    line_start(*sy, line_total(*sx))
-    av_field = left_place(inner, halo_wait(4))
+    at_row = lax.broadcasted_iota(jnp.int32, (8, 128), 0)
+    at_lane = lax.broadcasted_iota(jnp.int32, (8, 128), 1)
+    packed = jnp.where(at_row == at_lane, jnp.sum(partial, axis=1, keepdims=True), 0.0)
+    sums.start(jnp.sum(packed, axis=0, keepdims=True))
+    sums.middle()
+    halo_wait(4)
+    av_field = gathered(4, av_local)
     w_field = field_w[...]
-    totals = jnp.sum(line_total(*sy), axis=1, keepdims=True)
-    rz, zw, rv, vw, vav, zav = [totals[row : row + 1] for row in range(6)]
+    totals = sums.finish()
+    rz, zw, rv, vw, vav, zav = [totals[:, lane : lane + 1] for lane in range(6)]
     step_0 = rz / zw
     rho_1 = rz - step_0 * (rv + zw) + step_0 * step_0 * vw
     momentum = rho_1 / rz
@@ -456,34 +535,39 @@
         out_r[row] = final_r[8 * row : 8 * row + 7, :points]
 
     for turn in range(ROUNDS):
-        for slot in range(8):
-            halo_copy(turn, slot).wait_send()
-    for group in (*cx, *cy, sx, sy):
-        line_drain(*group)
+        for copy in halo_copies(turn):
+            copy.wait_send()
+    for lane in (*coarse, sums):
+        lane.drain()
 
 
 def local(n_gx, n_gy, right_side, stiff_coef, mass_coef, coarse_factor):
     elements = stiff_coef.shape[2]
     coarse_count, coarse_all = coarse_factor.shape
-    tables = constants(elements, coarse_count)
+    tables = {name: jnp.asarray(table) for name, table in constants(elements, coarse_count).items()}
+    tables.update(rhs=right_side, stiff=stiff_coef, mass=mass_coef, factor=coarse_factor)
+    operands = [tables[name] for name in OPERANDS]
     z_pad = round_up(7 * elements, 128)
     s_pad = round_up(10 * elements, 128)
     dma = pltpu.SemaphoreType.DMA
     single = jnp.float32
     whole = pl.BlockSpec(memory_space=pltpu.VMEM)
     shape = jax.ShapeDtypeStruct(right_side.shape, single)
+    lanes = []
+    for width in (coarse_all, coarse_all, 128):
+        for stage in stages_of(n_gx, n_gy):
+            size = stage_size(stage, n_gx, n_gy)
+            lanes += [pltpu.VMEM((size, 1, width), single), dma((size,)), dma((size,))]
     return pl.pallas_call(
-        functools.partial(kernel, n_gx, n_gy),
+        functools.partial(kernel, n_gx, n_gy, len(operands)),
         out_shape=(shape, shape),
-        in_specs=[whole] * (4 + len(tables)),
+        in_specs=[pl.BlockSpec(memory_space=pltpu.HBM)] * len(operands),
         out_specs=(whole, whole),
-        scratch_shapes=[
+        scratch_shapes=[pltpu.VMEM(operand.shape, operand.dtype) for operand in operands]
+        + [
+            dma((len(operands),)),
             pltpu.VMEM((ROUNDS, STACK, z_pad), single),
             pltpu.VMEM((ROUNDS, STACK, z_pad), single),
-            pltpu.VMEM((2, n_gx, 1, coarse_all), single),
-            pltpu.VMEM((2, n_gy, 1, coarse_all), single),
-            pltpu.VMEM((n_gx, 8, z_pad), single),
-            pltpu.VMEM((n_gy, 8, z_pad), single),
             pltpu.VMEM((z_pad, z_pad), jnp.bfloat16),
             pltpu.VMEM((z_pad, z_pad), jnp.bfloat16),
             pltpu.VMEM((SPEC, s_pad), single),
@@ -491,19 +575,12 @@
             pltpu.VMEM((OWN, z_pad), single),
             dma((ROUNDS, 8)),
             dma((ROUNDS, 8)),
-            dma((2, n_gx)),
-            dma((2, n_gx)),
-            dma((2, n_gy)),
-            dma((2, n_gy)),
-            dma((n_gx,)),
-            dma((n_gx,)),
-            dma((n_gy,)),
-            dma((n_gy,)),
-        ],
+        ]
+        + lanes,
         compiler_params=pltpu.CompilerParams(
             collective_id=0, has_side_effects=True, vmem_limit_bytes=40 * 1024 * 1024
         ),
-    )(right_side, stiff_coef, mass_coef, coarse_factor, *[jnp.asarray(table) for table in tables])
+    )(*operands)
 
 
 def solution(mesh):

time: 53 us -> 54.8 us (1.034)
  Pallas kernels: 33.4 us -> 35.2 us
    pallas_call x1, Pallas kernels: 33.4 us -> 35.2 us  [local(): pl.pallas_call(functools.partial(kernel, n_gx, n_gy, len(operands)), out_...]
where the time goes in v2:
time: 54.8 us; the launch traced here: 54.1 us
  Pallas kernels  35.2 us (64%)
  local copies, waits for them, and re-layouts  18.2 us (33%)
  between operations  0.68 us (1%)
    pallas_call x1, Pallas kernels, local(): pl.pallas_call(functools.partial(kernel, n_gx, n_gy, len(operands)), out_...  35.2 us
    unnamed x44, local copies, waits for them, and re-layouts  18.2 us

profile of v2, /device:TPU:0, one launch (start us, length us, event | category | flops | bytes accessed | tf_op | source)
XLA Modules:
  0.0 54.1 jit_solution(6930881456061866109)
XLA Ops:
  0.6 0.0 copy-start.18
  0.6 0.0 copy-start.17
  0.7 0.7 %copy-done.18 = f32[8,256]{1,0:T(8,128)S(1)} copy-done((f32[8,256]{1,0:T(8,128)S(1)}, f32[8,256]{1,0:T(8,128)}, u32[]{:S(2)}) %copy-start.18) | copy-done | bytes 8216
  1.3 0.0 copy-done.17
  1.3 0.0 copy-start
  1.3 0.9 %copy-done = f32[256,256]{1,0:T(8,128)S(1)} copy-done((f32[256,256]{1,0:T(8,128)S(1)}, f32[256,256]{1,0:T(8,128)}, u32[]{:S(2)}) %copy-start) | copy-done | bytes 262168
  2.3 0.0 copy-start.1
  2.3 0.9 %copy-done.1 = f32[256,256]{1,0:T(8,128)S(1)} copy-done((f32[256,256]{1,0:T(8,128)S(1)}, f32[256,256]{1,0:T(8,128)}, u32[]{:S(2)}) %copy-start.1) | copy-done | bytes 262168
  3.2 0.0 copy-start.2
  3.3 0.9 %copy-done.2 = bf16[160,480]{1,0:T(8,128)(2,1)S(1)} copy-done((bf16[160,480]{1,0:T(8,128)(2,1)S(1)}, bf16[160,480]{1,0:T(8,128)(2,1)}, u32[]{:S(2)}) %copy-start.2) | copy-done | bytes 153624
  4.2 0.0 copy-start.3
  4.2 0.9 %copy-done.3 = bf16[256,256]{1,0:T(8,128)(2,1)S(1)} copy-done((bf16[256,256]{1,0:T(8,128)(2,1)S(1)}, bf16[256,256]{1,0:T(8,128)(2,1)}, u32[]{:S(2)}) %copy-start.3) | copy-done | bytes 131096
  5.1 0.0 copy-start.4
  5.1 0.9 %copy-done.4 = bf16[256,256]{1,0:T(8,128)(2,1)S(1)} copy-done((bf16[256,256]{1,0:T(8,128)(2,1)S(1)}, bf16[256,256]{1,0:T(8,128)(2,1)}, u32[]{:S(2)}) %copy-start.4) | copy-done | bytes 131096
  6.0 0.9 %copy-done.5 = bf16[256,256]{1,0:T(8,128)(2,1)S(1)} copy-done((bf16[256,256]{1,0:T(8,128)(2,1)S(1)}, bf16[256,256]{1,0:T(8,128)(2,1)}, u32[]{:S(2)}) %copy-start.5) | copy-done | bytes 131096
  6.9 0.0 copy-start.6
  6.9 0.9 %copy-done.6 = bf16[256,256]{1,0:T(8,128)(2,1)S(1)} copy-done((bf16[256,256]{1,0:T(8,128)(2,1)S(1)}, bf16[256,256]{1,0:T(8,128)(2,1)}, u32[]{:S(2)}) %copy-start.6) | copy-done | bytes 131096
  7.8 0.9 %copy-done.7 = bf16[160,336]{1,0:T(8,128)(2,1)S(1)} copy-done((bf16[160,336]{1,0:T(8,128)(2,1)S(1)}, bf16[160,336]{1,0:T(8,128)(2,1)}, u32[]{:S(2)}) %copy-start.7) | copy-done | bytes 107544
  8.7 0.9 %copy-done.8 = f32[112,256]{1,0:T(8,128)S(1)} copy-done((f32[112,256]{1,0:T(8,128)S(1)}, f32[112,256]{1,0:T(8,128)}, u32[]{:S(2)}) %copy-start.8) | copy-done | bytes 114712
  9.6 0.9 %copy-done.9 = bf16[112,480]{1,0:T(8,128)(2,1)S(1)} copy-done((bf16[112,480]{1,0:T(8,128)(2,1)S(1)}, bf16[112,480]{1,0:T(8,128)(2,1)}, u32[]{:S(2)}) %copy-start.9) | copy-done | bytes 107544
  10.5 0.9 %copy-done.10 = f32[160,1]{1,0:T(8,128)S(1)} copy-done((f32[160,1]{1,0:T(8,128)S(1)}, f32[160,1]{1,0:T(8,128)}, u32[]{:S(2)}) %copy-start.10) | copy-done | bytes 664
  11.4 0.9 %copy-done.11 = bf16[160,192]{1,0:T(8,128)(2,1)S(1)} copy-done((bf16[160,192]{1,0:T(8,128)(2,1)S(1)}, bf16[160,192]{1,0:T(8,128)(2,1)}, u32[]{:S(2)}) %copy-start.11) | copy-done | bytes 61464
  12.3 0.9 %copy-done.12 = bf16[160,192]{1,0:T(8,128)(2,1)S(1)} copy-done((bf16[160,192]{1,0:T(8,128)(2,1)S(1)}, bf16[160,192]{1,0:T(8,128)(2,1)}, u32[]{:S(2)}) %copy-start.12) | copy-done | bytes 61464
  13.1 0.9 %copy-done.13 = f32[24,768]{1,0:T(8,128)S(1)} copy-done((f32[24,768]{1,0:T(8,128)S(1)}, f32[24,768]{1,0:T(8,128)}, u32[]{:S(2)}) %copy-start.13) | copy-done | bytes 73752
  14.0 0.8 %copy-done.14 = f32[7,7,168]{2,1,0:T(8,128)S(1)} copy-done((f32[7,7,168]{2,1,0:T(8,128)S(1)}, f32[7,7,168]{2,1,0:T(8,128)}, u32[]{:S(2)}) %copy-start.14) | copy-done | bytes 32952
  14.9 0.7 %copy-done.15 = bf16[64,96]{1,0:T(8,128)(2,1)S(1)} copy-done((bf16[64,96]{1,0:T(8,128)(2,1)S(1)}, bf16[64,96]{1,0:T(8,128)(2,1)}, u32[]{:S(2)}) %copy-start.15) | copy-done | bytes 12312
  15.6 0.7 %copy-done.16 = f32[8,256]{1,0:T(8,128)S(1)} copy-done((f32[8,256]{1,0:T(8,128)S(1)}, f32[8,256]{1,0:T(8,128)}, u32[]{:S(2)}) %copy-start.16) | copy-done | bytes 8216
  16.3 0.7 %copy-done.19 = f32[1,1,24]{2,1,0:T(1,128)S(1)} copy-done((f32[1,1,24]{2,1,0:T(1,128)S(1)}, f32[1,1,24]{2,1,0:T(1,128)}, u32[]{:S(2)}) %copy-start.19) | copy-done | bytes 120
  16.9 0.7 %copy-done.20 = f32[1,1,24]{2,1,0:T(1,128)S(1)} copy-done((f32[1,1,24]{2,1,0:T(1,128)S(1)}, f32[1,1,24]{2,1,0:T(1,128)}, u32[]{:S(2)}) %copy-start.20) | copy-done | bytes 120
  17.6 35.2 %shard_map.212 = (f32[7,7,168]{2,1,0:T(8,128)S(1)}, f32[7,7,168]{2,1,0:T(8,128)S(1)}) custom-call(f32[7,7,168]{2,1,0:T(8,128)S(1)} %copy-done.14, bf16[160,192]{1,0:T(8,128)(2,1)S(1)} %copy-done.12, f32[8,256]{1,0:T(8,128)S(1)} %copy-done.17, f32[8,256]{1,0:T(8,128)S(1)} %copy-done.16, f32[1,1,24]{2,1,0:T(1,128)S(1)} %copy-done.19, ...), custom_call_target="tpu_custom_call" | custom-call | tf_op jit(solution)/shard_map/pallas_call | solution.py:561
  52.8 0.6 %copy.25 = f32[7,7,168]{2,1,0:T(8,128)} copy(f32[7,7,168]{2,1,0:T(8,128)S(1)} %get-tuple-element.4) | data formatting | bytes 65856
  53.4 0.6 %copy.26 = f32[7,7,168]{2,1,0:T(8,128)} copy(f32[7,7,168]{2,1,0:T(8,128)S(1)} %get-tuple-element.5) | data formatting | bytes 65856
  (13 shorter events, 0.0 us)
Async XLA Ops:
  0.6 0.7 %copy-start.18 = (f32[8,256]{1,0:T(8,128)S(1)}, f32[8,256]{1,0:T(8,128)}, u32[]{:S(2)}) copy-start(f32[8,256]{1,0:T(8,128)} %constant.48.clone.refs_7_) | copy-start | bytes 24580
  0.6 0.7 %copy-start.17 = (f32[8,256]{1,0:T(8,128)S(1)}, f32[8,256]{1,0:T(8,128)}, u32[]{:S(2)}) copy-start(f32[8,256]{1,0:T(8,128)} %constant.49.clone.refs_2_) | copy-start | bytes 24580
  1.3 0.9 %copy-start = (f32[256,256]{1,0:T(8,128)S(1)}, f32[256,256]{1,0:T(8,128)}, u32[]{:S(2)}) copy-start(f32[256,256]{1,0:T(8,128)} %constant.45.clone.refs_10_) | copy-start | bytes 786436
  2.3 0.9 %copy-start.1 = (f32[256,256]{1,0:T(8,128)S(1)}, f32[256,256]{1,0:T(8,128)}, u32[]{:S(2)}) copy-start(f32[256,256]{1,0:T(8,128)} %constant.44.clone.refs_9_) | copy-start | bytes 786436
  3.2 0.9 %copy-start.2 = (bf16[160,480]{1,0:T(8,128)(2,1)S(1)}, bf16[160,480]{1,0:T(8,128)(2,1)}, u32[]{:S(2)}) copy-start(bf16[160,480]{1,0:T(8,128)(2,1)} %constant.37.clone.refs_17_) | copy-start | bytes 460804
  4.2 0.9 %copy-start.3 = (bf16[256,256]{1,0:T(8,128)(2,1)S(1)}, bf16[256,256]{1,0:T(8,128)(2,1)}, u32[]{:S(2)}) copy-start(bf16[256,256]{1,0:T(8,128)(2,1)} %constant.43.clone.refs_15_) | copy-start | bytes 393220
  5.1 0.9 %copy-start.4 = (bf16[256,256]{1,0:T(8,128)(2,1)S(1)}, bf16[256,256]{1,0:T(8,128)(2,1)}, u32[]{:S(2)}) copy-start(bf16[256,256]{1,0:T(8,128)(2,1)} %constant.42.clone.refs_14_) | copy-start | bytes 393220
  6.0 0.9 %copy-start.5 = (bf16[256,256]{1,0:T(8,128)(2,1)S(1)}, bf16[256,256]{1,0:T(8,128)(2,1)}, u32[]{:S(2)}) copy-start(bf16[256,256]{1,0:T(8,128)(2,1)} %constant.41.clone.refs_13_) | copy-start | bytes 393220
  6.9 0.9 %copy-start.6 = (bf16[256,256]{1,0:T(8,128)(2,1)S(1)}, bf16[256,256]{1,0:T(8,128)(2,1)}, u32[]{:S(2)}) copy-start(bf16[256,256]{1,0:T(8,128)(2,1)} %constant.40.clone.refs_12_) | copy-start | bytes 393220
  7.8 0.9 %copy-start.7 = (bf16[160,336]{1,0:T(8,128)(2,1)S(1)}, bf16[160,336]{1,0:T(8,128)(2,1)}, u32[]{:S(2)}) copy-start(bf16[160,336]{1,0:T(8,128)(2,1)} %constant.36.clone.refs_16_) | copy-start | bytes 322564
  8.7 0.9 %copy-start.8 = (f32[112,256]{1,0:T(8,128)S(1)}, f32[112,256]{1,0:T(8,128)}, u32[]{:S(2)}) copy-start(f32[112,256]{1,0:T(8,128)} %constant.46.clone.refs_8_) | copy-start | bytes 344068
  9.6 0.9 %copy-start.9 = (bf16[112,480]{1,0:T(8,128)(2,1)S(1)}, bf16[112,480]{1,0:T(8,128)(2,1)}, u32[]{:S(2)}) copy-start(bf16[112,480]{1,0:T(8,128)(2,1)} %constant.35.clone.refs_11_) | copy-start | bytes 322564
  10.5 0.9 %copy-start.10 = (f32[160,1]{1,0:T(8,128)S(1)}, f32[160,1]{1,0:T(8,128)}, u32[]{:S(2)}) copy-start(f32[160,1]{1,0:T(8,128)} %constant.50.clone.refs_19_) | copy-start | bytes 1924
  11.4 0.9 %copy-start.11 = (bf16[160,192]{1,0:T(8,128)(2,1)S(1)}, bf16[160,192]{1,0:T(8,128)(2,1)}, u32[]{:S(2)}) copy-start(bf16[160,192]{1,0:T(8,128)(2,1)} %constant.38.clone.refs_18_) | copy-start | bytes 184324
  12.3 0.9 %copy-start.12 = (bf16[160,192]{1,0:T(8,128)(2,1)S(1)}, bf16[160,192]{1,0:T(8,128)(2,1)}, u32[]{:S(2)}) copy-start(bf16[160,192]{1,0:T(8,128)(2,1)} %constant.34.clone.refs_1_) | copy-start | bytes 184324
  13.1 0.9 %copy-start.13 = (f32[24,768]{1,0:T(8,128)S(1)}, f32[24,768]{1,0:T(8,128)}, u32[]{:S(2)}) copy-start(f32[24,768]{1,0:T(8,128)} %constant.47.clone.refs_6_) | copy-start | bytes 221188
  14.0 0.8 %copy-start.14 = (f32[7,7,168]{2,1,0:T(8,128)S(1)}, f32[7,7,168]{2,1,0:T(8,128)}, u32[]{:S(2)}) copy-start(f32[7,7,168]{2,1,0:T(8,128)} %refs_0_.1) | copy-start | bytes 98788
  14.8 0.7 %copy-start.15 = (bf16[64,96]{1,0:T(8,128)(2,1)S(1)}, bf16[64,96]{1,0:T(8,128)(2,1)}, u32[]{:S(2)}) copy-start(bf16[64,96]{1,0:T(8,128)(2,1)} %constant.39.clone.refs_20_) | copy-start | bytes 36868
  15.6 0.7 %copy-start.16 = (f32[8,256]{1,0:T(8,128)S(1)}, f32[8,256]{1,0:T(8,128)}, u32[]{:S(2)}) copy-start(f32[8,256]{1,0:T(8,128)} %refs_3_.1) | copy-start | bytes 24580
  16.3 0.7 %copy-start.19 = (f32[1,1,24]{2,1,0:T(1,128)S(1)}, f32[1,1,24]{2,1,0:T(1,128)}, u32[]{:S(2)}) copy-start(f32[1,1,24]{2,1,0:T(1,128)} %refs_4_.1) | copy-start | bytes 292
  16.9 0.7 %copy-start.20 = (f32[1,1,24]{2,1,0:T(1,128)S(1)}, f32[1,1,24]{2,1,0:T(1,128)}, u32[]{:S(2)}) copy-start(f32[1,1,24]{2,1,0:T(1,128)} %refs_5_.1) | copy-start | bytes 292

commit v3 on v2

--- a/solution.py
+++ b/solution.py
@@ -29,7 +29,7 @@
 LAST = ((72, 0), (104, 2), (128, 4))
 OPERANDS = (
     "rhs", "pick_a", "segments", "factor", "stiff", "mass", "spread", "lines", "lam_all", "own_cols", "before_cols",
-    "spec_in", "win_h", "win_l", "back_h", "back_l", "spec_out", "pick_place", "plane", "plane_weight", "inner",
+    "spec_in", "window", "back", "spec_out", "pick_place", "plane", "plane_weight", "inner",
 )
 DIRECT = 64
 
@@ -137,20 +137,8 @@
     return pick, place
 
 
-def halves(matrix):
-    exact = np.asarray(matrix, np.float32)
-    high = exact.astype(jnp.bfloat16)
-    low = (exact - high.astype(np.float32)).astype(jnp.bfloat16)
-    return high, low
-
-
-def left_split(matrix):
-    high, low = halves(matrix)
-    return np.concatenate([high, low, high], axis=1)
-
-
-def left_exact(matrix):
-    return np.concatenate([np.asarray(matrix).astype(jnp.bfloat16)] * 3, axis=1)
+def thrice(matrix):
+    return np.concatenate([np.asarray(matrix, np.float32)] * 3, axis=1)
 
 
 def constants(elements, coarse_count):
@@ -204,22 +192,18 @@
     for row in range(coarse_count):
         length = points // coarse_count
         segments[row, row * length : (row + 1) * length] = 1.0
-    window_high, window_low = halves(window)
-    back_high, back_low = halves(window.T)
     inner = place_a.reshape(10, 10, STACK)[1:9, 1:9].reshape(OWN, STACK)
     inner = np.concatenate([inner[:, start : start + 8] for start, _ in LAST] + [np.zeros((OWN, 8))], axis=1)
     single = lambda value: np.asarray(value, np.float32)
     return {
-        "pick_a": left_exact(pick_a),
-        "spec_in": left_split(spectral_in),
-        "spec_out": left_split(spectral_out),
-        "pick_place": left_exact(pick_a @ place_s),
-        "plane": left_split(pick_a @ plane),
-        "inner": left_exact(inner),
-        "win_h": window_high,
-        "win_l": window_low,
-        "back_h": back_high,
-        "back_l": back_low,
+        "pick_a": thrice(pick_a),
+        "spec_in": thrice(spectral_in),
+        "spec_out": thrice(spectral_out),
+        "pick_place": thrice(pick_a @ place_s),
+        "plane": thrice(pick_a @ plane),
+        "inner": thrice(inner),
+        "window": single(window),
+        "back": single(window.T),
         "own_cols": single(own_cols),
         "before_cols": single(before_cols),
         "lam_all": single(lam_all),
@@ -239,16 +223,16 @@
     return jnp.dot(left, right, preferred_element_type=jnp.float32)
 
 
-def left_mul(matrix_ref, value):
+def left_mul(matrix, value):
     high, low = split_two(value)
-    return mul(matrix_ref[...], jnp.concatenate([high, high, low], axis=0))
-
-
-def left_place(matrix_ref, value):
+    return mul(matrix[...], jnp.concatenate([high, high, low], axis=0))
+
+
+def left_place(matrix, value):
     high = value.astype(jnp.bfloat16)
     rest = value - high.astype(jnp.float32)
     middle, low = split_two(rest)
-    return mul(matrix_ref[...], jnp.concatenate([high, middle, low], axis=0))
+    return mul(matrix[...], jnp.concatenate([high, middle, low], axis=0))
 
 
 def right_mul(value, high_ref, low_ref):
@@ -284,10 +268,13 @@
     load_sem, stack, sending, z_high, z_low, scale, first, field_w, halo_send, halo_recv = refs[
         2 * n_in + 2 : 2 * n_in + 12
     ]
-    lanes = refs[2 * n_in + 12 :]
+    spec_in, spec_out, pick_place, plane, inner, win_h, win_l, back_h, back_l = refs[
+        2 * n_in + 12 : 2 * n_in + 21
+    ]
+    lanes = refs[2 * n_in + 21 :]
     (
-        rhs, pick_a, segments, factor, stiff, mass, spread, lines, lam_all, own_cols, before_cols,
-        spec_in, win_h, win_l, back_h, back_l, spec_out, pick_place, plane, plane_weight, inner,
+        rhs, pick_a_f, segments, factor, stiff, mass, spread, lines, lam_all, own_cols, before_cols,
+        spec_in_f, window, back, spec_out_f, pick_place_f, plane_f, plane_weight, inner_f,
     ) = loaded
     loads = [
         pltpu.make_async_copy(source, target, load_sem.at[index])
@@ -298,8 +285,7 @@
 
     me_x, me_y = lax.axis_index("gx"), lax.axis_index("gy")
     points = rhs.shape[2]
-    z_pad = win_h.shape[0]
-    s_pad = win_h.shape[1]
+    z_pad, s_pad = window.shape
     stages = stages_of(n_gx, n_gy)
 
     def beside(off_x, off_y):
@@ -424,7 +410,7 @@
     for row in range(7):
         first[pl.ds(8 * row, 7), pl.ds(0, points)] = rhs[row]
     right = first[...]
-    rows = left_place(pick_a, right)
+    rows = left_place(pick_a_f[...].astype(jnp.bfloat16), right)
     pl.semaphore_wait(barrier, greeted)
     halo_start(0, rows)
     coarse_start(0, right)
@@ -453,6 +439,22 @@
 
     for load in loads[11:]:
         load.wait()
+
+    def three_parts(source, target):
+        high, low = split_two(source[...])
+        column = lax.broadcasted_iota(jnp.int32, source.shape, 1)
+        third = source.shape[1] // 3
+        middle = (column >= third) & (column < 2 * third)
+        target[...] = jnp.where(
+            middle, low.astype(jnp.float32), high.astype(jnp.float32)
+        ).astype(jnp.bfloat16)
+
+    for source, target in ((spec_in_f, spec_in), (spec_out_f, spec_out), (plane_f, plane)):
+        three_parts(source, target)
+    for source, target in ((pick_place_f, pick_place), (inner_f, inner)):
+        target[...] = source[...].astype(jnp.bfloat16)
+    win_h[...], win_l[...] = split_two(window[...])
+    back_h[...], back_l[...] = split_two(back[...])
 
     def schwarz(rows):
         spectral = right_mul(left_mul(spec_in, rows), win_h, win_l) * scale[...]
@@ -576,9 +578,15 @@
             dma((ROUNDS, 8)),
             dma((ROUNDS, 8)),
         ]
+        + [
+            pltpu.VMEM(tables[name].shape, jnp.bfloat16)
+            for name in (
+                "spec_in", "spec_out", "pick_place", "plane", "inner", "window", "window", "back", "back",
+            )
+        ]
         + lanes,
         compiler_params=pltpu.CompilerParams(
-            collective_id=0, has_side_effects=True, vmem_limit_bytes=40 * 1024 * 1024
+            collective_id=0, has_side_effects=True, vmem_limit_bytes=60 * 1024 * 1024
         ),
     )(*operands)
 

time: 54.8 us -> 36.9 us (0.67)
  local copies, waits for them, and re-layouts: 18.2 us -> 2.09 us
  Pallas kernels: 35.2 us -> 34 us
    unnamed x44 -> x4, local copies, waits for them, and re-layouts: 18.2 us -> 2.09 us
    pallas_call x1, Pallas kernels: 35.2 us -> 34 us  [local(): pl.pallas_call(functools.partial(kernel, n_gx, n_gy, len(operands)), out_...]
where the time goes in v3:
time: 36.9 us; the launch traced here: 36.7 us
  Pallas kernels  34 us (92%)
  local copies, waits for them, and re-layouts  2.09 us (6%)
  between operations  0.65 us (2%)
    pallas_call x1, Pallas kernels, local(): pl.pallas_call(functools.partial(kernel, n_gx, n_gy, len(operands)), out_...  34 us
    unnamed x4, local copies, waits for them, and re-layouts  2.09 us

profile of v3, /device:TPU:0, one launch (start us, length us, event | category | flops | bytes accessed | tf_op | source)
XLA Modules:
  0.0 36.7 jit_solution(5273782745258806761)
XLA Ops:
  0.6 34.0 %shard_map.194 = (f32[7,7,168]{2,1,0:T(8,128)}, f32[7,7,168]{2,1,0:T(8,128)}) custom-call(f32[7,7,168]{2,1,0:T(8,128)} %refs_0_.1, f32[160,192]{1,0:T(8,128)} %constant.30.clone.refs_1_, f32[8,256]{1,0:T(8,128)} %constant.43.clone.refs_2_, f32[8,256]{1,0:T(8,128)} %refs_3_.1, f32[1,1,24]{2,1,0:T(1,128)} %refs_4_.1, f32[1,1,24]{2,1,0:T(1,128)} %refs_5_.1, ...), custom_call_target="tpu_custom_call" | custom-call | tf_op jit(solution)/shard_map/pallas_call | solution.py:563
  34.6 0.0 copy-start
  34.6 1.5 %copy.23 = f32[7,7,168]{2,1,0:T(8,128)} copy(f32[7,7,168]{2,1,0:T(8,128)} %get-tuple-element.4) | data formatting | bytes 65856
  36.1 0.0 copy-done
  36.1 0.6 %copy.24 = f32[7,7,168]{2,1,0:T(8,128)} copy(f32[7,7,168]{2,1,0:T(8,128)S(1)} %copy-done) | data formatting | bytes 65856
Async XLA Ops:
  34.6 1.5 %copy-start = (f32[7,7,168]{2,1,0:T(8,128)S(1)}, f32[7,7,168]{2,1,0:T(8,128)}, u32[]{:S(2)}) copy-start(f32[7,7,168]{2,1,0:T(8,128)} %get-tuple-element.5) | copy-start | bytes 98788

commit v4 on v3

--- a/solution.py
+++ b/solution.py
@@ -26,7 +26,10 @@
 )
 STACK = 160
 SPEC = 112
+PACKED = ((0, 24), (24, 24), (48, 24), (72, 24), (96, 8), (104, 8), (112, 8), (120, 8))
+MESSAGE = 128
 LAST = ((72, 0), (104, 2), (128, 4))
+LAST_PACKED = {0: (8, 16), 2: (56, 16), 4: (96, 8)}
 OPERANDS = (
     "rhs", "pick_a", "segments", "factor", "stiff", "mass", "spread", "lines", "lam_all", "own_cols", "before_cols",
     "spec_in", "window", "back", "spec_out", "pick_place", "plane", "plane_weight", "inner",
@@ -130,6 +133,8 @@
         pairs = [(one, two) for one in pairs_x for two in pairs_y]
         if off_x == 0 and off_y != 0:
             pairs = [(one, two) for two in pairs_y for one in pairs_x]
+        if off_x != 0 and off_y != 0:
+            pairs = pairs + pairs
         for (from_x, to_x), (from_y, to_y) in pairs:
             pick[row, from_x * size_from + from_y] = 1.0
             place[to_x * size_to + to_y, row] = 1.0
@@ -265,13 +270,13 @@
     sources = refs[:n_in]
     out_x, out_r = refs[n_in : n_in + 2]
     loaded = refs[n_in + 2 : 2 * n_in + 2]
-    load_sem, stack, sending, z_high, z_low, scale, first, field_w, halo_send, halo_recv = refs[
-        2 * n_in + 2 : 2 * n_in + 12
+    load_sem, arrived, sending, own_rows, z_high, z_low, scale, first, field_w, halo_send, halo_recv = refs[
+        2 * n_in + 2 : 2 * n_in + 13
     ]
     spec_in, spec_out, pick_place, plane, inner, win_h, win_l, back_h, back_l = refs[
-        2 * n_in + 12 : 2 * n_in + 21
+        2 * n_in + 13 : 2 * n_in + 22
     ]
-    lanes = refs[2 * n_in + 21 :]
+    lanes = refs[2 * n_in + 22 :]
     (
         rhs, pick_a_f, segments, factor, stiff, mass, spread, lines, lam_all, own_cols, before_cols,
         spec_in_f, window, back, spec_out_f, pick_place_f, plane_f, plane_weight, inner_f,
@@ -320,7 +325,7 @@
         off_x, off_y, _, _ = SLOTS[slot]
         return pltpu.make_async_remote_copy(
             src_ref=sending.at[turn, pl.ds(start, rows)],
-            dst_ref=stack.at[turn, pl.ds(start, rows)],
+            dst_ref=arrived.at[turn, pl.ds(start, rows)],
             send_sem=halo_send.at[turn, slot],
             recv_sem=halo_recv.at[turn, slot],
             device_id=beside(-off_x, -off_y),
@@ -329,25 +334,66 @@
 
     def halo_copies(turn):
         if turn == ROUNDS - 1:
-            return [halo_copy(turn, slot, start, 8) for start, slot in LAST]
-        return [halo_copy(turn, slot, SLOTS[slot][2], SLOTS[slot][3]) for slot in range(8)]
+            return [halo_copy(turn, slot, *LAST_PACKED[slot]) for _, slot in LAST]
+        return [halo_copy(turn, slot, *PACKED[slot]) for slot in range(8)]
+
+    tile_row = lax.broadcasted_iota(jnp.int32, (8, 128), 0)
+    tile_lane = lax.broadcasted_iota(jnp.int32, (8, 128), 1)
 
     def halo_start(turn, rows):
-        sending[turn] = rows
+        for slot, (_, _, start, count) in enumerate(SLOTS):
+            at = PACKED[slot][0]
+            if count == 8:
+                part = rows[start : start + 8]
+                sending[turn, pl.ds(at, 8)] = jnp.where(tile_row < 4, part[:, :128], part[:, 128:])
+            else:
+                sending[turn, pl.ds(at, 16)] = rows[start : start + 16, :128]
+                sending[turn, pl.ds(at + 16, 8)] = rows[start : start + 8, 128:] + pltpu.roll(
+                    rows[start + 8 : start + 16, 128:], 64, 1
+                )
         for copy in halo_copies(turn):
             copy.start()
-        stack[turn, pl.ds(0, OWN)] = rows[:OWN]
+        own_rows[turn] = rows[:OWN]
+
+    def left_half(tile):
+        return jnp.where(tile_lane < 64, tile, 0.0)
+
+    def corner_rows(turn, slot):
+        tile = arrived[turn, pl.ds(PACKED[slot][0], 8)]
+        upper = jnp.where(tile_row < 4, tile, 0.0)
+        return jnp.concatenate([upper, jnp.where(tile_row < 4, 0.0, tile)], axis=1)
+
+    def first_rows(turn, slot):
+        at = PACKED[slot][0]
+        tail = arrived[turn, pl.ds(at + 16, 8)]
+        return jnp.concatenate([arrived[turn, pl.ds(at, 8)], left_half(tail)], axis=1)
+
+    def second_rows(turn, slot):
+        at = PACKED[slot][0]
+        tail = pltpu.roll(arrived[turn, pl.ds(at + 16, 8)], 64, 1)
+        return jnp.concatenate([arrived[turn, pl.ds(at + 8, 8)], left_half(tail)], axis=1)
 
     def halo_wait(turn):
         for copy in halo_copies(turn):
             copy.wait_recv()
 
+    def stack(turn):
+        parts = [own_rows[turn]]
+        for slot in range(4):
+            parts += [first_rows(turn, slot), second_rows(turn, slot)]
+        parts += [corner_rows(turn, slot) for slot in range(4, 8)]
+        return jnp.concatenate(parts, axis=0)
+
+    def halo_drain(turn):
+        for copy in halo_copies(turn):
+            copy.wait_send()
+
     def slot_of(stage, off_x, off_y):
         at_x, at_y = beside(off_x, off_y)
         return {"x": at_x, "y": at_y, "xy": at_x * n_gy + at_y}[stage]
 
     class Lane:
-        def __init__(self, buffers):
+        def __init__(self, stages, buffers):
             self.legs = [(stage,) + tuple(buffers[3 * at : 3 * at + 3]) for at, stage in enumerate(stages)]
 
         def copy(self, leg, off_x, off_y, slot):
@@ -385,9 +431,8 @@
                 mine = slot_of(leg[0], 0, 0)
                 each_offset(leg[0], lambda x, y: self.copy(leg, x, y, mine).wait_send())
 
-    per_lane = 3 * len(stages)
-    coarse = [Lane(lanes[:per_lane]), Lane(lanes[per_lane : 2 * per_lane])]
-    sums = Lane(lanes[2 * per_lane :])
+    coarse = [Lane(("x", "y"), lanes[:6]), Lane(("x", "y"), lanes[6:12])]
+    sums = Lane(stages, lanes[12:])
 
     point = lax.broadcasted_iota(jnp.int32, (OWN, z_pad), 0)
     at_x, at_y = point // 8, point % 8
@@ -471,30 +516,32 @@
     def precondition(turn):
         coarse[turn].middle()
         halo_wait(2 * turn)
-        result = schwarz(stack[2 * turn])
+        result = schwarz(stack(2 * turn))
         halo_start(2 * turn + 1, result)
         plate = coarse_finish(turn)
-        stack[2 * turn + 1, pl.ds(0, OWN)] = result[:OWN] + plate
+        own_rows[2 * turn + 1] = result[:OWN] + plate
+        halo_drain(2 * turn)
+        coarse[turn].drain()
 
     def dot_line(left, other):
         return jnp.sum(left * other, axis=0, keepdims=True)
 
     def gathered(turn, own):
-        parts = [stack[turn, pl.ds(start, 8)] for start, _ in LAST]
+        parts = [second_rows(turn, 0), second_rows(turn, 2), corner_rows(turn, 4)]
         return own + left_place(inner, jnp.concatenate(parts + [jnp.zeros_like(parts[0])], axis=0))
 
     owned = (at_x < 7) & (at_y < 7)
 
     precondition(0)
     halo_wait(1)
-    z_field, w_rows = element(stack[1])
+    z_field, w_rows = element(stack(1))
     halo_start(2, w_rows)
     w_local = w_rows[:OWN]
     coarse_start(1, w_local)
     precondition(1)
     field_w[...] = gathered(2, w_local)
     halo_wait(3)
-    v_field, av_rows = element(stack[3])
+    v_field, av_rows = element(stack(3))
     halo_start(4, av_rows)
     av_local = av_rows[:OWN]
     partial = jnp.concatenate(
@@ -514,6 +561,9 @@
     packed = jnp.where(at_row == at_lane, jnp.sum(partial, axis=1, keepdims=True), 0.0)
     sums.start(jnp.sum(packed, axis=0, keepdims=True))
     sums.middle()
+    for turn in (1, 3, 4):
+        halo_drain(turn)
+    sums.drain()
     halo_wait(4)
     av_field = gathered(4, av_local)
     w_field = field_w[...]
@@ -536,11 +586,16 @@
         out_x[row] = final_x[8 * row : 8 * row + 7, :points]
         out_r[row] = final_r[8 * row : 8 * row + 7, :points]
 
-    for turn in range(ROUNDS):
-        for copy in halo_copies(turn):
-            copy.wait_send()
-    for lane in (*coarse, sums):
-        lane.drain()
+
+def move(from_x, from_r, to_x, to_r, sem):
+    copies = [
+        pltpu.make_async_copy(from_x, to_x, sem.at[0]),
+        pltpu.make_async_copy(from_r, to_r, sem.at[1]),
+    ]
+    for copy in copies:
+        copy.start()
+    for copy in copies:
+        copy.wait()
 
 
 def local(n_gx, n_gy, right_side, stiff_coef, mass_coef, coarse_factor):
@@ -556,11 +611,12 @@
     whole = pl.BlockSpec(memory_space=pltpu.VMEM)
     shape = jax.ShapeDtypeStruct(right_side.shape, single)
     lanes = []
-    for width in (coarse_all, coarse_all, 128):
-        for stage in stages_of(n_gx, n_gy):
+    two = ("x", "y")
+    for width, stages in ((coarse_all, two), (coarse_all, two), (128, stages_of(n_gx, n_gy))):
+        for stage in stages:
             size = stage_size(stage, n_gx, n_gy)
             lanes += [pltpu.VMEM((size, 1, width), single), dma((size,)), dma((size,))]
-    return pl.pallas_call(
+    result = pl.pallas_call(
         functools.partial(kernel, n_gx, n_gy, len(operands)),
         out_shape=(shape, shape),
         in_specs=[pl.BlockSpec(memory_space=pltpu.HBM)] * len(operands),
@@ -568,8 +624,9 @@
         scratch_shapes=[pltpu.VMEM(operand.shape, operand.dtype) for operand in operands]
         + [
             dma((len(operands),)),
-            pltpu.VMEM((ROUNDS, STACK, z_pad), single),
-            pltpu.VMEM((ROUNDS, STACK, z_pad), single),
+            pltpu.VMEM((ROUNDS, MESSAGE, 128), single),
+            pltpu.VMEM((ROUNDS, MESSAGE, 128), single),
+            pltpu.VMEM((ROUNDS, OWN, z_pad), single),
             pltpu.VMEM((z_pad, z_pad), jnp.bfloat16),
             pltpu.VMEM((z_pad, z_pad), jnp.bfloat16),
             pltpu.VMEM((SPEC, s_pad), single),
@@ -589,6 +646,14 @@
             collective_id=0, has_side_effects=True, vmem_limit_bytes=60 * 1024 * 1024
         ),
     )(*operands)
+    return pl.pallas_call(
+        move,
+        out_shape=(shape, shape),
+        in_specs=[pl.BlockSpec(memory_space=pltpu.HBM)] * 2,
+        out_specs=(pl.BlockSpec(memory_space=pltpu.HBM),) * 2,
+        scratch_shapes=[dma((2,))],
+        compiler_params=pltpu.CompilerParams(vmem_limit_bytes=60 * 1024 * 1024),
+    )(*result)
 
 
 def solution(mesh):

time: 36.9 us -> 38 us (1.030)
  Pallas kernels: 34 us -> 37.2 us
  local copies, waits for them, and re-layouts: 2.09 us -> 0 us
    pallas_call x0 -> x1, Pallas kernels: none -> 4.6 us  [local(): pl.pallas_call(move, out_shape=(shape, shape), in_specs=[pl.BlockSpec(mem...]
    unnamed x4 -> x0, local copies, waits for them, and re-layouts: 2.09 us -> none
    pallas_call x1, Pallas kernels: 34 us -> 32.6 us  [local(): pl.pallas_call(functools.partial(kernel, n_gx, n_gy, len(operands)), out_...]
where the time goes in v4:
time: 38 us; the launch traced here: 37.8 us
  Pallas kernels  37.2 us (98%)
  between operations  0.64 us (2%)
    pallas_call x1, Pallas kernels, local(): pl.pallas_call(functools.partial(kernel, n_gx, n_gy, len(operands)), out_...  32.6 us
    pallas_call x1, Pallas kernels, local(): pl.pallas_call(move, out_shape=(shape, shape), in_specs=[pl.BlockSpec(mem...  4.6 us

profile of v4, /device:TPU:0, one launch (start us, length us, event | category | flops | bytes accessed | tf_op | source)
XLA Modules:
  0.0 37.8 jit_solution(7039797253467589044)
XLA Ops:
  0.6 32.6 %shard_map.194 = (f32[7,7,168]{2,1,0:T(8,128)}, f32[7,7,168]{2,1,0:T(8,128)}) custom-call(f32[7,7,168]{2,1,0:T(8,128)} %refs_0_.1, f32[160,192]{1,0:T(8,128)} %constant.30.clone.refs_1_, f32[8,256]{1,0:T(8,128)} %constant.43.clone.refs_2_, f32[8,256]{1,0:T(8,128)} %refs_3_.1, f32[1,1,24]{2,1,0:T(1,128)} %refs_4_.1, f32[1,1,24]{2,1,0:T(1,128)} %refs_5_.1, ...), custom_call_target="tpu_custom_call" | custom-call | tf_op jit(solution)/shard_map/pallas_call | solution.py:619
  33.2 4.6 %shard_map.195 = (f32[7,7,168]{2,1,0:T(8,128)}, f32[7,7,168]{2,1,0:T(8,128)}) custom-call(f32[7,7,168]{2,1,0:T(8,128)} %get-tuple-element.4.from_x, f32[7,7,168]{2,1,0:T(8,128)} %get-tuple-element.5.from_r), custom_call_target="tpu_custom_call" | custom-call | tf_op jit(solution)/shard_map/pallas_call | solution.py:649

commit v5 on v4

--- a/solution.py
+++ b/solution.py
@@ -31,8 +31,9 @@
 LAST = ((72, 0), (104, 2), (128, 4))
 LAST_PACKED = {0: (8, 16), 2: (56, 16), 4: (96, 8)}
 OPERANDS = (
-    "rhs", "pick_a", "segments", "factor", "stiff", "mass", "spread", "lines", "lam_all", "own_cols", "before_cols",
-    "spec_in", "window", "back", "spec_out", "pick_place", "plane", "plane_weight", "inner",
+    "rhs", "pick_a", "segments", "factor",
+    "stiff", "mass", "spread", "lines", "lam_all", "spec_in", "window", "back", "spec_out",
+    "own_cols", "before_cols", "pick_place", "plane", "plane_weight", "inner",
 )
 DIRECT = 64
 
@@ -278,8 +279,9 @@
     ]
     lanes = refs[2 * n_in + 22 :]
     (
-        rhs, pick_a_f, segments, factor, stiff, mass, spread, lines, lam_all, own_cols, before_cols,
-        spec_in_f, window, back, spec_out_f, pick_place_f, plane_f, plane_weight, inner_f,
+        rhs, pick_a_f, segments, factor,
+        stiff, mass, spread, lines, lam_all, spec_in_f, window, back, spec_out_f,
+        own_cols, before_cols, pick_place_f, plane_f, plane_weight, inner_f,
     ) = loaded
     loads = [
         pltpu.make_async_copy(source, target, load_sem.at[index])
@@ -335,7 +337,7 @@
     def halo_copies(turn):
         if turn == ROUNDS - 1:
             return [halo_copy(turn, slot, *LAST_PACKED[slot]) for _, slot in LAST]
-        return [halo_copy(turn, slot, *PACKED[slot]) for slot in range(8)]
+        return [halo_copy(turn, slot, *PACKED[slot]) for slot in (4, 5, 6, 7, 0, 1, 2, 3)]
 
     tile_row = lax.broadcasted_iota(jnp.int32, (8, 128), 0)
     tile_lane = lax.broadcasted_iota(jnp.int32, (8, 128), 1)
@@ -460,30 +462,14 @@
     halo_start(0, rows)
     coarse_start(0, right)
 
-    for load in loads[4:11]:
+    for load in loads[4:13]:
         load.wait()
 
-    def spread_out(coef):
-        flat = jnp.dot(
-            jnp.broadcast_to(coef[0], (8, coef.shape[2])), spread[...],
+    def spread_out(coef, start, size):
+        return jnp.dot(
+            jnp.broadcast_to(coef[0], (8, coef.shape[2])), spread[:, start : start + size],
             precision=exact_mode, preferred_element_type=jnp.float32,
         )[0:1]
-        return flat[:, :s_pad], flat[:, s_pad : s_pad + z_pad], flat[:, s_pad + z_pad :]
-
-    stiff_s, stiff_own, stiff_before = spread_out(stiff)
-    mass_s, mass_own, mass_before = spread_out(mass)
-    weight_own, weight_before = lines[0:1, :z_pad], lines[1:2, :z_pad]
-    line_stiff = stiff_own * weight_own + stiff_before * weight_before
-    line_mass = mass_own * weight_own + mass_before * weight_before
-    scale[...] = 1.0 / (stiff_s * lam_all[...] + (mass_s + lines[2:3, :s_pad]))
-    diagonal = lax.broadcasted_iota(jnp.int32, (z_pad, z_pad), 0) == lax.broadcasted_iota(
-        jnp.int32, (z_pad, z_pad), 1
-    )
-    along = own_cols[...] * stiff_own + before_cols[...] * stiff_before
-    z_high[...], z_low[...] = split_two(along + jnp.where(diagonal, line_mass, 0.0))
-
-    for load in loads[11:]:
-        load.wait()
 
     def three_parts(source, target):
         high, low = split_two(source[...])
@@ -494,16 +480,29 @@
             middle, low.astype(jnp.float32), high.astype(jnp.float32)
         ).astype(jnp.bfloat16)
 
-    for source, target in ((spec_in_f, spec_in), (spec_out_f, spec_out), (plane_f, plane)):
-        three_parts(source, target)
-    for source, target in ((pick_place_f, pick_place), (inner_f, inner)):
-        target[...] = source[...].astype(jnp.bfloat16)
+    stiff_s, mass_s = spread_out(stiff, 0, s_pad), spread_out(mass, 0, s_pad)
+    scale[...] = 1.0 / (stiff_s * lam_all[...] + (mass_s + lines[2:3, :s_pad]))
+    three_parts(spec_in_f, spec_in)
+    three_parts(spec_out_f, spec_out)
     win_h[...], win_l[...] = split_two(window[...])
     back_h[...], back_l[...] = split_two(back[...])
 
-    def schwarz(rows):
-        spectral = right_mul(left_mul(spec_in, rows), win_h, win_l) * scale[...]
-        return left_mul(spec_out, right_mul(spectral, back_h, back_l))
+    def prepare_elements():
+        for load in loads[13:]:
+            load.wait()
+        stiff_own, stiff_before = spread_out(stiff, s_pad, z_pad), spread_out(stiff, s_pad + z_pad, z_pad)
+        mass_own, mass_before = spread_out(mass, s_pad, z_pad), spread_out(mass, s_pad + z_pad, z_pad)
+        weight_own, weight_before = lines[0:1, :z_pad], lines[1:2, :z_pad]
+        line_mass = mass_own * weight_own + mass_before * weight_before
+        diagonal = lax.broadcasted_iota(jnp.int32, (z_pad, z_pad), 0) == lax.broadcasted_iota(
+            jnp.int32, (z_pad, z_pad), 1
+        )
+        along = own_cols[...] * stiff_own + before_cols[...] * stiff_before
+        z_high[...], z_low[...] = split_two(along + jnp.where(diagonal, line_mass, 0.0))
+        three_parts(plane_f, plane)
+        for source, target in ((pick_place_f, pick_place), (inner_f, inner)):
+            target[...] = source[...].astype(jnp.bfloat16)
+        return stiff_own * weight_own + stiff_before * weight_before
 
     def element(rows):
         wide = left_place(pick_place, rows)
@@ -514,9 +513,10 @@
         return field, result
 
     def precondition(turn):
+        halo_wait(2 * turn)
+        spectral = right_mul(left_mul(spec_in, stack(2 * turn)), win_h, win_l) * scale[...]
         coarse[turn].middle()
-        halo_wait(2 * turn)
-        result = schwarz(stack(2 * turn))
+        result = left_mul(spec_out, right_mul(spectral, back_h, back_l))
         halo_start(2 * turn + 1, result)
         plate = coarse_finish(turn)
         own_rows[2 * turn + 1] = result[:OWN] + plate
@@ -533,6 +533,7 @@
     owned = (at_x < 7) & (at_y < 7)
 
     precondition(0)
+    line_stiff = prepare_elements()
     halo_wait(1)
     z_field, w_rows = element(stack(1))
     halo_start(2, w_rows)
@@ -587,15 +588,9 @@
         out_r[row] = final_r[8 * row : 8 * row + 7, :points]
 
 
-def move(from_x, from_r, to_x, to_r, sem):
-    copies = [
-        pltpu.make_async_copy(from_x, to_x, sem.at[0]),
-        pltpu.make_async_copy(from_r, to_r, sem.at[1]),
-    ]
-    for copy in copies:
-        copy.start()
-    for copy in copies:
-        copy.wait()
+def move(from_x, from_r, to_x, to_r):
+    to_x[...] = from_x[...]
+    to_r[...] = from_r[...]
 
 
 def local(n_gx, n_gy, right_side, stiff_coef, mass_coef, coarse_factor):
@@ -649,9 +644,8 @@
     return pl.pallas_call(
         move,
         out_shape=(shape, shape),
-        in_specs=[pl.BlockSpec(memory_space=pltpu.HBM)] * 2,
-        out_specs=(pl.BlockSpec(memory_space=pltpu.HBM),) * 2,
-        scratch_shapes=[dma((2,))],
+        in_specs=[whole] * 2,
+        out_specs=(whole, whole),
         compiler_params=pltpu.CompilerParams(vmem_limit_bytes=60 * 1024 * 1024),
     )(*result)
 

time: 38 us -> 34.8 us (0.916)
  Pallas kernels: 37.2 us -> 34 us
    pallas_call x1, Pallas kernels: 4.6 us -> 1.5 us  [local(): pl.pallas_call(move, out_shape=(shape, shape), in_specs=[whole] * 2, out_...]
where the time goes in v5:
time: 34.8 us; the launch traced here: 34.7 us
  Pallas kernels  34 us (98%)
  between operations  0.64 us (2%)
    pallas_call x1, Pallas kernels, local(): pl.pallas_call(functools.partial(kernel, n_gx, n_gy, len(operands)), out_...  32.5 us
    pallas_call x1, Pallas kernels, local(): pl.pallas_call(move, out_shape=(shape, shape), in_specs=[whole] * 2, out_...  1.5 us

profile of v5, /device:TPU:0, one launch (start us, length us, event | category | flops | bytes accessed | tf_op | source)
XLA Modules:
  0.0 34.7 jit_solution(14289061948303824013)
XLA Ops:
  0.6 32.5 %shard_map.194 = (f32[7,7,168]{2,1,0:T(8,128)}, f32[7,7,168]{2,1,0:T(8,128)}) custom-call(f32[7,7,168]{2,1,0:T(8,128)} %refs_0_.1, f32[160,192]{1,0:T(8,128)} %constant.30.clone.refs_1_, f32[8,256]{1,0:T(8,128)} %constant.43.clone.refs_2_, f32[8,256]{1,0:T(8,128)} %refs_3_.1, f32[1,1,24]{2,1,0:T(1,128)} %refs_4_.1, f32[1,1,24]{2,1,0:T(1,128)} %refs_5_.1, ...), custom_call_target="tpu_custom_call" | custom-call | tf_op jit(solution)/shard_map/pallas_call | solution.py:614
  33.2 1.5 %shard_map.195 = (f32[7,7,168]{2,1,0:T(8,128)}, f32[7,7,168]{2,1,0:T(8,128)}) custom-call(f32[7,7,168]{2,1,0:T(8,128)} %get-tuple-element.4.from_x, f32[7,7,168]{2,1,0:T(8,128)} %get-tuple-element.5.from_r), custom_call_target="tpu_custom_call" | custom-call | tf_op jit(solution)/shard_map/pallas_call | solution.py:644

commit v6 on v5

--- a/solution.py
+++ b/solution.py
@@ -32,10 +32,10 @@
 LAST_PACKED = {0: (8, 16), 2: (56, 16), 4: (96, 8)}
 OPERANDS = (
     "rhs", "pick_a", "segments", "factor",
-    "stiff", "mass", "spread", "lines", "lam_all", "spec_in", "window", "back", "spec_out",
+    "stiff", "mass", "spread", "lines", "lam_all", "spec_in", "win_h", "win_l", "back_h", "back_l", "spec_out",
     "own_cols", "before_cols", "pick_place", "plane", "plane_weight", "inner",
 )
-DIRECT = 64
+STAGES = ("x", "y")
 
 
 def legendre_pair(position, degree):
@@ -143,8 +143,20 @@
     return pick, place
 
 
-def thrice(matrix):
-    return np.concatenate([np.asarray(matrix, np.float32)] * 3, axis=1)
+def halves(matrix):
+    exact = np.asarray(matrix, np.float32)
+    high = exact.astype(jnp.bfloat16)
+    low = (exact - high.astype(np.float32)).astype(jnp.bfloat16)
+    return high, low
+
+
+def left_split(matrix):
+    high, low = halves(matrix)
+    return np.concatenate([high, low, high], axis=1)
+
+
+def left_exact(matrix):
+    return np.concatenate([np.asarray(matrix).astype(jnp.bfloat16)] * 3, axis=1)
 
 
 def constants(elements, coarse_count):
@@ -200,16 +212,20 @@
         segments[row, row * length : (row + 1) * length] = 1.0
     inner = place_a.reshape(10, 10, STACK)[1:9, 1:9].reshape(OWN, STACK)
     inner = np.concatenate([inner[:, start : start + 8] for start, _ in LAST] + [np.zeros((OWN, 8))], axis=1)
+    window_high, window_low = halves(window)
+    back_high, back_low = halves(window.T)
     single = lambda value: np.asarray(value, np.float32)
     return {
-        "pick_a": thrice(pick_a),
-        "spec_in": thrice(spectral_in),
-        "spec_out": thrice(spectral_out),
-        "pick_place": thrice(pick_a @ place_s),
-        "plane": thrice(pick_a @ plane),
-        "inner": thrice(inner),
-        "window": single(window),
-        "back": single(window.T),
+        "pick_a": left_exact(pick_a),
+        "spec_in": left_split(spectral_in),
+        "spec_out": left_split(spectral_out),
+        "pick_place": left_exact(pick_a @ place_s),
+        "plane": left_split(pick_a @ plane),
+        "inner": left_exact(inner),
+        "win_h": window_high,
+        "win_l": window_low,
+        "back_h": back_high,
+        "back_l": back_low,
         "own_cols": single(own_cols),
         "before_cols": single(before_cols),
         "lam_all": single(lam_all),
@@ -259,12 +275,8 @@
         lax.fori_loop(1, count, body, 0)
 
 
-def stages_of(n_gx, n_gy):
-    return ("xy",) if n_gx * n_gy <= DIRECT else ("x", "y")
-
-
 def stage_size(stage, n_gx, n_gy):
-    return {"x": n_gx, "y": n_gy, "xy": n_gx * n_gy}[stage]
+    return {"x": n_gx, "y": n_gy}[stage]
 
 
 def kernel(n_gx, n_gy, n_in, *refs):
@@ -274,14 +286,11 @@
     load_sem, arrived, sending, own_rows, z_high, z_low, scale, first, field_w, halo_send, halo_recv = refs[
         2 * n_in + 2 : 2 * n_in + 13
     ]
-    spec_in, spec_out, pick_place, plane, inner, win_h, win_l, back_h, back_l = refs[
-        2 * n_in + 13 : 2 * n_in + 22
-    ]
-    lanes = refs[2 * n_in + 22 :]
+    lanes = refs[2 * n_in + 13 :]
     (
-        rhs, pick_a_f, segments, factor,
-        stiff, mass, spread, lines, lam_all, spec_in_f, window, back, spec_out_f,
-        own_cols, before_cols, pick_place_f, plane_f, plane_weight, inner_f,
+        rhs, pick_a, segments, factor,
+        stiff, mass, spread, lines, lam_all, spec_in, win_h, win_l, back_h, back_l, spec_out,
+        own_cols, before_cols, pick_place, plane, plane_weight, inner,
     ) = loaded
     loads = [
         pltpu.make_async_copy(source, target, load_sem.at[index])
@@ -292,19 +301,13 @@
 
     me_x, me_y = lax.axis_index("gx"), lax.axis_index("gy")
     points = rhs.shape[2]
-    z_pad, s_pad = window.shape
-    stages = stages_of(n_gx, n_gy)
+    z_pad, s_pad = win_h.shape
 
     def beside(off_x, off_y):
         return (lax.rem(me_x + off_x + n_gx, n_gx), lax.rem(me_y + off_y + n_gy, n_gy))
 
     def each_offset(stage, act):
-        if stage == "xy":
-            for off_x in range(n_gx):
-                for off_y in range(n_gy):
-                    if off_x or off_y:
-                        act(off_x, off_y)
-        elif stage == "x":
+        if stage == "x":
             each_other(n_gx, lambda step: act(step, 0))
         else:
             each_other(n_gy, lambda step: act(0, step))
@@ -315,13 +318,12 @@
         pl.semaphore_signal(barrier, inc=1, device_id=beside(off_x, off_y), device_id_type=MESH)
 
     greeted = 0
-    for stage in stages:
+    for stage in STAGES:
         each_offset(stage, greet)
         greeted += stage_size(stage, n_gx, n_gy) - 1
-    if stages != ("xy",):
-        for off_x, off_y, _, _ in SLOTS[4:]:
-            greet(off_x, off_y)
-        greeted += 4
+    for off_x, off_y, _, _ in SLOTS[4:]:
+        greet(off_x, off_y)
+        greeted += 1
 
     def halo_copy(turn, slot, start, rows):
         off_x, off_y, _, _ = SLOTS[slot]
@@ -392,19 +394,19 @@
 
     def slot_of(stage, off_x, off_y):
         at_x, at_y = beside(off_x, off_y)
-        return {"x": at_x, "y": at_y, "xy": at_x * n_gy + at_y}[stage]
+        return {"x": at_x, "y": at_y}[stage]
 
     class Lane:
-        def __init__(self, stages, buffers):
-            self.legs = [(stage,) + tuple(buffers[3 * at : 3 * at + 3]) for at, stage in enumerate(stages)]
+        def __init__(self, buffers):
+            self.legs = [(stage,) + tuple(buffers[3 * at : 3 * at + 3]) for at, stage in enumerate(STAGES)]
 
         def copy(self, leg, off_x, off_y, slot):
             _, buf, send, recv = leg
             return pltpu.make_async_remote_copy(
                 src_ref=buf.at[slot],
                 dst_ref=buf.at[slot],
-                send_sem=send.at[off_x * n_gy + off_y if leg[0] == "xy" else off_x + off_y],
-                recv_sem=recv.at[off_x * n_gy + off_y if leg[0] == "xy" else off_x + off_y],
+                send_sem=send.at[off_x + off_y],
+                recv_sem=recv.at[off_x + off_y],
                 device_id=beside(off_x, off_y),
                 device_id_type=MESH,
             )
@@ -433,8 +435,8 @@
                 mine = slot_of(leg[0], 0, 0)
                 each_offset(leg[0], lambda x, y: self.copy(leg, x, y, mine).wait_send())
 
-    coarse = [Lane(("x", "y"), lanes[:6]), Lane(("x", "y"), lanes[6:12])]
-    sums = Lane(stages, lanes[12:])
+    coarse = [Lane(lanes[:6]), Lane(lanes[6:12])]
+    sums = Lane(lanes[12:])
 
     point = lax.broadcasted_iota(jnp.int32, (OWN, z_pad), 0)
     at_x, at_y = point // 8, point % 8
@@ -457,12 +459,12 @@
     for row in range(7):
         first[pl.ds(8 * row, 7), pl.ds(0, points)] = rhs[row]
     right = first[...]
-    rows = left_place(pick_a_f[...].astype(jnp.bfloat16), right)
+    rows = left_place(pick_a, right)
     pl.semaphore_wait(barrier, greeted)
     halo_start(0, rows)
     coarse_start(0, right)
 
-    for load in loads[4:13]:
+    for load in loads[4:15]:
         load.wait()
 
     def spread_out(coef, start, size):
@@ -471,24 +473,11 @@
             precision=exact_mode, preferred_element_type=jnp.float32,
         )[0:1]
 
-    def three_parts(source, target):
-        high, low = split_two(source[...])
-        column = lax.broadcasted_iota(jnp.int32, source.shape, 1)
-        third = source.shape[1] // 3
-        middle = (column >= third) & (column < 2 * third)
-        target[...] = jnp.where(
-            middle, low.astype(jnp.float32), high.astype(jnp.float32)
-        ).astype(jnp.bfloat16)
-
     stiff_s, mass_s = spread_out(stiff, 0, s_pad), spread_out(mass, 0, s_pad)
     scale[...] = 1.0 / (stiff_s * lam_all[...] + (mass_s + lines[2:3, :s_pad]))
-    three_parts(spec_in_f, spec_in)
-    three_parts(spec_out_f, spec_out)
-    win_h[...], win_l[...] = split_two(window[...])
-    back_h[...], back_l[...] = split_two(back[...])
 
     def prepare_elements():
-        for load in loads[13:]:
+        for load in loads[15:]:
             load.wait()
         stiff_own, stiff_before = spread_out(stiff, s_pad, z_pad), spread_out(stiff, s_pad + z_pad, z_pad)
         mass_own, mass_before = spread_out(mass, s_pad, z_pad), spread_out(mass, s_pad + z_pad, z_pad)
@@ -499,9 +488,6 @@
         )
         along = own_cols[...] * stiff_own + before_cols[...] * stiff_before
         z_high[...], z_low[...] = split_two(along + jnp.where(diagonal, line_mass, 0.0))
-        three_parts(plane_f, plane)
-        for source, target in ((pick_place_f, pick_place), (inner_f, inner)):
-            target[...] = source[...].astype(jnp.bfloat16)
         return stiff_own * weight_own + stiff_before * weight_before
 
     def element(rows):
@@ -606,9 +592,8 @@
     whole = pl.BlockSpec(memory_space=pltpu.VMEM)
     shape = jax.ShapeDtypeStruct(right_side.shape, single)
     lanes = []
-    two = ("x", "y")
-    for width, stages in ((coarse_all, two), (coarse_all, two), (128, stages_of(n_gx, n_gy))):
-        for stage in stages:
+    for width in (coarse_all, coarse_all, 128):
+        for stage in STAGES:
             size = stage_size(stage, n_gx, n_gy)
             lanes += [pltpu.VMEM((size, 1, width), single), dma((size,)), dma((size,))]
     result = pl.pallas_call(
@@ -630,12 +615,6 @@
             dma((ROUNDS, 8)),
             dma((ROUNDS, 8)),
         ]
-        + [
-            pltpu.VMEM(tables[name].shape, jnp.bfloat16)
-            for name in (
-                "spec_in", "spec_out", "pick_place", "plane", "inner", "window", "window", "back", "back",
-            )
-        ]
         + lanes,
         compiler_params=pltpu.CompilerParams(
             collective_id=0, has_side_effects=True, vmem_limit_bytes=60 * 1024 * 1024

time: 34.8 us -> 36.1 us (1.037)
  Pallas kernels: 34 us -> 35.3 us
    pallas_call x1, Pallas kernels: 32.5 us -> 33.8 us  [local(): pl.pallas_call(functools.partial(kernel, n_gx, n_gy, len(operands)), out_...]
where the time goes in v6:
time: 36.1 us; the launch traced here: 36 us
  Pallas kernels  35.3 us (98%)
  between operations  0.64 us (2%)
    pallas_call x1, Pallas kernels, local(): pl.pallas_call(functools.partial(kernel, n_gx, n_gy, len(operands)), out_...  33.8 us
    pallas_call x1, Pallas kernels, local(): pl.pallas_call(move, out_shape=(shape, shape), in_specs=[whole] * 2, out_...  1.5 us

profile of v6, /device:TPU:0, one launch (start us, length us, event | category | flops | bytes accessed | tf_op | source)
XLA Modules:
  0.0 36.0 jit_solution(13805325289655391799)
XLA Ops:
  0.6 33.8 %shard_map.212 = (f32[7,7,168]{2,1,0:T(8,128)}, f32[7,7,168]{2,1,0:T(8,128)}) custom-call(f32[7,7,168]{2,1,0:T(8,128)} %refs_0_.1, bf16[160,192]{1,0:T(8,128)(2,1)} %constant.34.clone.refs_1_, f32[8,256]{1,0:T(8,128)} %constant.49.clone.refs_2_, f32[8,256]{1,0:T(8,128)} %refs_3_.1, f32[1,1,24]{2,1,0:T(1,128)} %refs_4_.1, f32[1,1,24]{2,1,0:T(1,128)} %refs_5_.1, ...), custom_call_target="tpu_custom_call" | custom-call | tf_op jit(solution)/shard_map/pallas_call | solution.py:599
  34.5 1.5 %shard_map.213 = (f32[7,7,168]{2,1,0:T(8,128)}, f32[7,7,168]{2,1,0:T(8,128)}) custom-call(f32[7,7,168]{2,1,0:T(8,128)} %get-tuple-element.4.from_x, f32[7,7,168]{2,1,0:T(8,128)} %get-tuple-element.5.from_r), custom_call_target="tpu_custom_call" | custom-call | tf_op jit(solution)/shard_map/pallas_call | solution.py:623

commit v7 on v6

--- a/solution.py
+++ b/solution.py
@@ -32,10 +32,11 @@
 LAST_PACKED = {0: (8, 16), 2: (56, 16), 4: (96, 8)}
 OPERANDS = (
     "rhs", "pick_a", "segments", "factor",
-    "stiff", "mass", "spread", "lines", "lam_all", "spec_in", "win_h", "win_l", "back_h", "back_l", "spec_out",
-    "own_cols", "before_cols", "pick_place", "plane", "plane_weight", "inner",
+    "stiff", "mass", "spread", "lines", "lam_all", "spec_own", "spec_in", "win_h", "win_l", "back_h", "back_l", "spec_out",
+    "own_cols", "before_cols", "pick_own", "pick_place", "plane", "plane_weight", "inner",
 )
 STAGES = ("x", "y")
+DIRECT = 64
 
 
 def legendre_pair(position, degree):
@@ -217,9 +218,11 @@
     single = lambda value: np.asarray(value, np.float32)
     return {
         "pick_a": left_exact(pick_a),
-        "spec_in": left_split(spectral_in),
+        "spec_in": left_split(spectral_in[:, OWN:]),
+        "spec_own": left_split(spectral_in[:, :OWN]),
         "spec_out": left_split(spectral_out),
-        "pick_place": left_exact(pick_a @ place_s),
+        "pick_place": left_exact((pick_a @ place_s)[:, OWN:]),
+        "pick_own": left_exact((pick_a @ place_s)[:, :OWN]),
         "plane": left_split(pick_a @ plane),
         "inner": left_exact(inner),
         "win_h": window_high,
@@ -259,7 +262,9 @@
 
 def right_mul(value, high_ref, low_ref):
     high, low = split_two(value)
-    return mul(high, high_ref[...]) + (mul(high, low_ref[...]) + mul(low, high_ref[...]))
+    both = mul(jnp.concatenate([high, low], axis=0), high_ref[...])
+    rows = value.shape[0]
+    return both[:rows] + (mul(high, low_ref[...]) + both[rows:])
 
 
 def each_other(count, act):
@@ -276,21 +281,25 @@
 
 
 def stage_size(stage, n_gx, n_gy):
-    return {"x": n_gx, "y": n_gy}[stage]
+    return {"x": n_gx, "y": n_gy, "xy": n_gx * n_gy}[stage]
+
+
+def last_stages(n_gx, n_gy):
+    return ("xy",) if n_gx * n_gy <= DIRECT else STAGES
 
 
 def kernel(n_gx, n_gy, n_in, *refs):
     sources = refs[:n_in]
-    out_x, out_r = refs[n_in : n_in + 2]
-    loaded = refs[n_in + 2 : 2 * n_in + 2]
+    out = refs[n_in]
+    loaded = refs[n_in + 1 : 2 * n_in + 1]
     load_sem, arrived, sending, own_rows, z_high, z_low, scale, first, field_w, halo_send, halo_recv = refs[
-        2 * n_in + 2 : 2 * n_in + 13
+        2 * n_in + 1 : 2 * n_in + 12
     ]
-    lanes = refs[2 * n_in + 13 :]
+    lanes = refs[2 * n_in + 12 :]
     (
         rhs, pick_a, segments, factor,
-        stiff, mass, spread, lines, lam_all, spec_in, win_h, win_l, back_h, back_l, spec_out,
-        own_cols, before_cols, pick_place, plane, plane_weight, inner,
+        stiff, mass, spread, lines, lam_all, spec_own, spec_in, win_h, win_l, back_h, back_l, spec_out,
+        own_cols, before_cols, pick_own, pick_place, plane, plane_weight, inner,
     ) = loaded
     loads = [
         pltpu.make_async_copy(source, target, load_sem.at[index])
@@ -307,7 +316,12 @@
         return (lax.rem(me_x + off_x + n_gx, n_gx), lax.rem(me_y + off_y + n_gy, n_gy))
 
     def each_offset(stage, act):
-        if stage == "x":
+        if stage == "xy":
+            for off_x in range(n_gx):
+                for off_y in range(n_gy):
+                    if off_x or off_y:
+                        act(off_x, off_y)
+        elif stage == "x":
             each_other(n_gx, lambda step: act(step, 0))
         else:
             each_other(n_gy, lambda step: act(0, step))
@@ -318,12 +332,13 @@
         pl.semaphore_signal(barrier, inc=1, device_id=beside(off_x, off_y), device_id_type=MESH)
 
     greeted = 0
-    for stage in STAGES:
+    for stage in last_stages(n_gx, n_gy):
         each_offset(stage, greet)
         greeted += stage_size(stage, n_gx, n_gy) - 1
-    for off_x, off_y, _, _ in SLOTS[4:]:
-        greet(off_x, off_y)
-        greeted += 1
+    if last_stages(n_gx, n_gy) == STAGES:
+        for off_x, off_y, _, _ in SLOTS[4:]:
+            greet(off_x, off_y)
+            greeted += 1
 
     def halo_copy(turn, slot, start, rows):
         off_x, off_y, _, _ = SLOTS[slot]
@@ -382,7 +397,7 @@
             copy.wait_recv()
 
     def stack(turn):
-        parts = [own_rows[turn]]
+        parts = []
         for slot in range(4):
             parts += [first_rows(turn, slot), second_rows(turn, slot)]
         parts += [corner_rows(turn, slot) for slot in range(4, 8)]
@@ -394,19 +409,20 @@
 
     def slot_of(stage, off_x, off_y):
         at_x, at_y = beside(off_x, off_y)
-        return {"x": at_x, "y": at_y}[stage]
+        return {"x": at_x, "y": at_y, "xy": at_x * n_gy + at_y}[stage]
 
     class Lane:
-        def __init__(self, buffers):
-            self.legs = [(stage,) + tuple(buffers[3 * at : 3 * at + 3]) for at, stage in enumerate(STAGES)]
+        def __init__(self, stages, buffers):
+            self.legs = [(stage,) + tuple(buffers[3 * at : 3 * at + 3]) for at, stage in enumerate(stages)]
 
         def copy(self, leg, off_x, off_y, slot):
-            _, buf, send, recv = leg
+            stage, buf, send, recv = leg
+            index = off_x * n_gy + off_y if stage == "xy" else off_x + off_y
             return pltpu.make_async_remote_copy(
                 src_ref=buf.at[slot],
                 dst_ref=buf.at[slot],
-                send_sem=send.at[off_x + off_y],
-                recv_sem=recv.at[off_x + off_y],
+                send_sem=send.at[index],
+                recv_sem=recv.at[index],
                 device_id=beside(off_x, off_y),
                 device_id_type=MESH,
             )
@@ -435,8 +451,8 @@
                 mine = slot_of(leg[0], 0, 0)
                 each_offset(leg[0], lambda x, y: self.copy(leg, x, y, mine).wait_send())
 
-    coarse = [Lane(lanes[:6]), Lane(lanes[6:12])]
-    sums = Lane(lanes[12:])
+    coarse = [Lane(STAGES, lanes[:6]), Lane(STAGES, lanes[6:12])]
+    sums = Lane(last_stages(n_gx, n_gy), lanes[12:])
 
     point = lax.broadcasted_iota(jnp.int32, (OWN, z_pad), 0)
     at_x, at_y = point // 8, point % 8
@@ -464,7 +480,7 @@
     halo_start(0, rows)
     coarse_start(0, right)
 
-    for load in loads[4:15]:
+    for load in loads[4:16]:
         load.wait()
 
     def spread_out(coef, start, size):
@@ -477,7 +493,7 @@
     scale[...] = 1.0 / (stiff_s * lam_all[...] + (mass_s + lines[2:3, :s_pad]))
 
     def prepare_elements():
-        for load in loads[15:]:
+        for load in loads[16:]:
             load.wait()
         stiff_own, stiff_before = spread_out(stiff, s_pad, z_pad), spread_out(stiff, s_pad + z_pad, z_pad)
         mass_own, mass_before = spread_out(mass, s_pad, z_pad), spread_out(mass, s_pad + z_pad, z_pad)
@@ -490,8 +506,10 @@
         z_high[...], z_low[...] = split_two(along + jnp.where(diagonal, line_mass, 0.0))
         return stiff_own * weight_own + stiff_before * weight_before
 
-    def element(rows):
-        wide = left_place(pick_place, rows)
+    def element(turn):
+        held = left_place(pick_own, own_rows[turn])
+        halo_wait(turn)
+        wide = held + left_place(pick_place, stack(turn))
         field = wide[:OWN]
         result = left_mul(plane, field * line_stiff) + plane_weight[...] * right_mul(
             wide, z_high, z_low
@@ -499,8 +517,9 @@
         return field, result
 
     def precondition(turn):
+        held = left_mul(spec_own, own_rows[2 * turn])
         halo_wait(2 * turn)
-        spectral = right_mul(left_mul(spec_in, stack(2 * turn)), win_h, win_l) * scale[...]
+        spectral = right_mul(held + left_mul(spec_in, stack(2 * turn)), win_h, win_l) * scale[...]
         coarse[turn].middle()
         result = left_mul(spec_out, right_mul(spectral, back_h, back_l))
         halo_start(2 * turn + 1, result)
@@ -520,15 +539,13 @@
 
     precondition(0)
     line_stiff = prepare_elements()
-    halo_wait(1)
-    z_field, w_rows = element(stack(1))
+    z_field, w_rows = element(1)
     halo_start(2, w_rows)
     w_local = w_rows[:OWN]
     coarse_start(1, w_local)
     precondition(1)
     field_w[...] = gathered(2, w_local)
-    halo_wait(3)
-    v_field, av_rows = element(stack(3))
+    v_field, av_rows = element(3)
     halo_start(4, av_rows)
     av_local = av_rows[:OWN]
     partial = jnp.concatenate(
@@ -569,14 +586,15 @@
     next_image = (w_field - step_0 * av_field) + momentum * w_field
     final_x = step_0 * z_field + step_1 * next_dir
     final_r = (right - step_0 * w_field) - step_1 * next_image
+    out[0] = final_x
+    out[1] = final_r
+
+
+def move(both, to_x, to_r):
+    points = to_x.shape[2]
     for row in range(7):
-        out_x[row] = final_x[8 * row : 8 * row + 7, :points]
-        out_r[row] = final_r[8 * row : 8 * row + 7, :points]
-
-
-def move(from_x, from_r, to_x, to_r):
-    to_x[...] = from_x[...]
-    to_r[...] = from_r[...]
+        to_x[row] = both[0, pl.ds(8 * row, 7), pl.ds(0, points)]
+        to_r[row] = both[1, pl.ds(8 * row, 7), pl.ds(0, points)]
 
 
 def local(n_gx, n_gy, right_side, stiff_coef, mass_coef, coarse_factor):
@@ -592,15 +610,16 @@
     whole = pl.BlockSpec(memory_space=pltpu.VMEM)
     shape = jax.ShapeDtypeStruct(right_side.shape, single)
     lanes = []
-    for width in (coarse_all, coarse_all, 128):
-        for stage in STAGES:
+    last = last_stages(n_gx, n_gy)
+    for width, stages in ((coarse_all, STAGES), (coarse_all, STAGES), (128, last)):
+        for stage in stages:
             size = stage_size(stage, n_gx, n_gy)
             lanes += [pltpu.VMEM((size, 1, width), single), dma((size,)), dma((size,))]
     result = pl.pallas_call(
         functools.partial(kernel, n_gx, n_gy, len(operands)),
-        out_shape=(shape, shape),
+        out_shape=jax.ShapeDtypeStruct((2, OWN, z_pad), single),
         in_specs=[pl.BlockSpec(memory_space=pltpu.HBM)] * len(operands),
-        out_specs=(whole, whole),
+        out_specs=whole,
         scratch_shapes=[pltpu.VMEM(operand.shape, operand.dtype) for operand in operands]
         + [
             dma((len(operands),)),
@@ -623,10 +642,10 @@
     return pl.pallas_call(
         move,
         out_shape=(shape, shape),
-        in_specs=[whole] * 2,
+        in_specs=[whole],
         out_specs=(whole, whole),
         compiler_params=pltpu.CompilerParams(vmem_limit_bytes=60 * 1024 * 1024),
-    )(*result)
+    )(result)
 
 
 def solution(mesh):

time: 36.1 us -> 35 us (0.970)
  Pallas kernels: 35.3 us -> 34.2 us
    pallas_call x1, Pallas kernels: 33.8 us -> 32.7 us  [local(): pl.pallas_call(functools.partial(kernel, n_gx, n_gy, len(operands)), out_...]
where the time goes in v7:
time: 35 us; the launch traced here: 34.9 us
  Pallas kernels  34.2 us (98%)
  between operations  0.64 us (2%)
    pallas_call x1, Pallas kernels, local(): pl.pallas_call(functools.partial(kernel, n_gx, n_gy, len(operands)), out_...  32.7 us
    pallas_call x1, Pallas kernels, local(): pl.pallas_call(move, out_shape=(shape, shape), in_specs=[whole], out_spec...  1.56 us

profile of v7, /device:TPU:0, one launch (start us, length us, event | category | flops | bytes accessed | tf_op | source)
XLA Modules:
  0.0 34.9 jit_solution(3318056457426011337)
XLA Ops:
  0.6 32.7 %shard_map.230.both = f32[2,64,256]{2,1,0:T(8,128)} custom-call(f32[7,7,168]{2,1,0:T(8,128)} %refs_0_.1, bf16[160,192]{1,0:T(8,128)(2,1)} %constant.36.clone.refs_1_.refs_18_, f32[8,256]{1,0:T(8,128)} %constant.52.clone.refs_2_, f32[8,256]{1,0:T(8,128)} %refs_3_.1, f32[1,1,24]{2,1,0:T(1,128)} %refs_4_.1, f32[1,1,24]{2,1,0:T(1,128)} %refs_5_.1, ...), custom_call_target="tpu_custom_call" | custom-call | tf_op jit(solution)/shard_map/pallas_call | solution.py:618
  33.3 1.6 %shard_map.231 = (f32[7,7,168]{2,1,0:T(8,128)}, f32[7,7,168]{2,1,0:T(8,128)}) custom-call(f32[2,64,256]{2,1,0:T(8,128)} %shard_map.230.both), custom_call_target="tpu_custom_call" | custom-call | tf_op jit(solution)/shard_map/pallas_call | solution.py:642

commit v8 on v7

--- a/solution.py
+++ b/solution.py
@@ -451,8 +451,10 @@
                 mine = slot_of(leg[0], 0, 0)
                 each_offset(leg[0], lambda x, y: self.copy(leg, x, y, mine).wait_send())
 
-    coarse = [Lane(STAGES, lanes[:6]), Lane(STAGES, lanes[6:12])]
-    sums = Lane(last_stages(n_gx, n_gy), lanes[12:])
+    ways = last_stages(n_gx, n_gy)
+    each = 3 * len(ways)
+    coarse = [Lane(ways, lanes[:each]), Lane(ways, lanes[each : 2 * each])]
+    sums = Lane(ways, lanes[2 * each :])
 
     point = lax.broadcasted_iota(jnp.int32, (OWN, z_pad), 0)
     at_x, at_y = point // 8, point % 8
@@ -610,9 +612,8 @@
     whole = pl.BlockSpec(memory_space=pltpu.VMEM)
     shape = jax.ShapeDtypeStruct(right_side.shape, single)
     lanes = []
-    last = last_stages(n_gx, n_gy)
-    for width, stages in ((coarse_all, STAGES), (coarse_all, STAGES), (128, last)):
-        for stage in stages:
+    for width in (coarse_all, coarse_all, 128):
+        for stage in last_stages(n_gx, n_gy):
             size = stage_size(stage, n_gx, n_gy)
             lanes += [pltpu.VMEM((size, 1, width), single), dma((size,)), dma((size,))]
     result = pl.pallas_call(

time: 35 us -> 35.6 us (1.017)
  Pallas kernels: 34.2 us -> 34.8 us
    pallas_call x1, Pallas kernels: 32.7 us -> 33.2 us  [local(): pl.pallas_call(functools.partial(kernel, n_gx, n_gy, len(operands)), out_...]
where the time goes in v8:
time: 35.6 us; the launch traced here: 35.4 us
  Pallas kernels  34.8 us (98%)
  between operations  0.64 us (2%)
    pallas_call x1, Pallas kernels, local(): pl.pallas_call(functools.partial(kernel, n_gx, n_gy, len(operands)), out_...  33.2 us
    pallas_call x1, Pallas kernels, local(): pl.pallas_call(move, out_shape=(shape, shape), in_specs=[whole], out_spec...  1.56 us

profile of v8, /device:TPU:0, one launch (start us, length us, event | category | flops | bytes accessed | tf_op | source)
XLA Modules:
  0.0 35.4 jit_solution(4239935511000849048)
XLA Ops:
  0.6 33.2 %shard_map.230.both = f32[2,64,256]{2,1,0:T(8,128)} custom-call(f32[7,7,168]{2,1,0:T(8,128)} %refs_0_.1, bf16[160,192]{1,0:T(8,128)(2,1)} %constant.36.clone.refs_1_.refs_18_, f32[8,256]{1,0:T(8,128)} %constant.52.clone.refs_2_, f32[8,256]{1,0:T(8,128)} %refs_3_.1, f32[1,1,24]{2,1,0:T(1,128)} %refs_4_.1, f32[1,1,24]{2,1,0:T(1,128)} %refs_5_.1, ...), custom_call_target="tpu_custom_call" | custom-call | tf_op jit(solution)/shard_map/pallas_call | solution.py:619
  33.9 1.6 %shard_map.231 = (f32[7,7,168]{2,1,0:T(8,128)}, f32[7,7,168]{2,1,0:T(8,128)}) custom-call(f32[2,64,256]{2,1,0:T(8,128)} %shard_map.230.both), custom_call_target="tpu_custom_call" | custom-call | tf_op jit(solution)/shard_map/pallas_call | solution.py:643

commit v9 on v7

--- a/solution.py
+++ b/solution.py
@@ -305,7 +305,7 @@
         pltpu.make_async_copy(source, target, load_sem.at[index])
         for index, (source, target) in enumerate(zip(sources, loaded))
     ]
-    for load in loads:
+    for load in loads[:4]:
         load.start()
 
     me_x, me_y = lax.axis_index("gx"), lax.axis_index("gy")
@@ -362,6 +362,8 @@
     def halo_start(turn, rows):
         for slot, (_, _, start, count) in enumerate(SLOTS):
             at = PACKED[slot][0]
+            if turn == ROUNDS - 1 and slot not in LAST_PACKED:
+                continue
             if count == 8:
                 part = rows[start : start + 8]
                 sending[turn, pl.ds(at, 8)] = jnp.where(tile_row < 4, part[:, :128], part[:, 128:])
@@ -480,6 +482,8 @@
     halo_start(0, rows)
     coarse_start(0, right)
 
+    for load in loads[4:]:
+        load.start()
     for load in loads[4:16]:
         load.wait()
 

time: 35 us -> 35 us (level)
  no operation moved by 1% of the time
where the time goes in v9:
time: 35 us; the launch traced here: 34.8 us
  Pallas kernels  34.2 us (98%)
  between operations  0.64 us (2%)
    pallas_call x1, Pallas kernels, local(): pl.pallas_call(functools.partial(kernel, n_gx, n_gy, len(operands)), out_...  32.6 us
    pallas_call x1, Pallas kernels, local(): pl.pallas_call(move, out_shape=(shape, shape), in_specs=[whole], out_spec...  1.56 us

profile of v9, /device:TPU:0, one launch (start us, length us, event | category | flops | bytes accessed | tf_op | source)
XLA Modules:
  0.0 34.8 jit_solution(15201617468773380753)
XLA Ops:
  0.6 32.6 %shard_map.230.both = f32[2,64,256]{2,1,0:T(8,128)} custom-call(f32[7,7,168]{2,1,0:T(8,128)} %refs_0_.1, bf16[160,192]{1,0:T(8,128)(2,1)} %constant.36.clone.refs_1_.refs_18_, f32[8,256]{1,0:T(8,128)} %constant.52.clone.refs_2_, f32[8,256]{1,0:T(8,128)} %refs_3_.1, f32[1,1,24]{2,1,0:T(1,128)} %refs_4_.1, f32[1,1,24]{2,1,0:T(1,128)} %refs_5_.1, ...), custom_call_target="tpu_custom_call" | custom-call | tf_op jit(solution)/shard_map/pallas_call | solution.py:622
  33.3 1.6 %shard_map.231 = (f32[7,7,168]{2,1,0:T(8,128)}, f32[7,7,168]{2,1,0:T(8,128)}) custom-call(f32[2,64,256]{2,1,0:T(8,128)} %shard_map.230.both), custom_call_target="tpu_custom_call" | custom-call | tf_op jit(solution)/shard_map/pallas_call | solution.py:646

commit v10 on v9

--- a/solution.py
+++ b/solution.py
@@ -156,8 +156,8 @@
     return np.concatenate([high, low, high], axis=1)
 
 
-def left_exact(matrix):
-    return np.concatenate([np.asarray(matrix).astype(jnp.bfloat16)] * 3, axis=1)
+def left_whole(matrix):
+    return np.concatenate([np.asarray(matrix).astype(jnp.bfloat16)] * 2, axis=1)
 
 
 def constants(elements, coarse_count):
@@ -217,14 +217,14 @@
     back_high, back_low = halves(window.T)
     single = lambda value: np.asarray(value, np.float32)
     return {
-        "pick_a": left_exact(pick_a),
+        "pick_a": left_whole(pick_a),
         "spec_in": left_split(spectral_in[:, OWN:]),
         "spec_own": left_split(spectral_in[:, :OWN]),
         "spec_out": left_split(spectral_out),
-        "pick_place": left_exact((pick_a @ place_s)[:, OWN:]),
-        "pick_own": left_exact((pick_a @ place_s)[:, :OWN]),
+        "pick_place": left_whole((pick_a @ place_s)[:, OWN:]),
+        "pick_own": left_whole((pick_a @ place_s)[:, :OWN]),
         "plane": left_split(pick_a @ plane),
-        "inner": left_exact(inner),
+        "inner": left_whole(inner),
         "win_h": window_high,
         "win_l": window_low,
         "back_h": back_high,
@@ -254,10 +254,7 @@
 
 
 def left_place(matrix, value):
-    high = value.astype(jnp.bfloat16)
-    rest = value - high.astype(jnp.float32)
-    middle, low = split_two(rest)
-    return mul(matrix[...], jnp.concatenate([high, middle, low], axis=0))
+    return mul(matrix[...], jnp.concatenate(split_two(value), axis=0))
 
 
 def right_mul(value, high_ref, low_ref):
@@ -576,7 +573,9 @@
     av_field = gathered(4, av_local)
     w_field = field_w[...]
     totals = sums.finish()
-    rz, zw, rv, vw, vav, zav = [totals[:, lane : lane + 1] for lane in range(6)]
+    rz, zw, rv, vw, vav, zav = [
+        jnp.broadcast_to(totals[:, lane : lane + 1], (1, z_pad)) for lane in range(6)
+    ]
     step_0 = rz / zw
     rho_1 = rz - step_0 * (rv + zw) + step_0 * step_0 * vw
     momentum = rho_1 / rz

time: 35 us -> 34.7 us (level)
  Pallas kernels: 34.2 us -> 33.8 us
    pallas_call x1, Pallas kernels: 32.6 us -> 32.2 us  [local(): pl.pallas_call(functools.partial(kernel, n_gx, n_gy, len(operands)), out_...]
where the time goes in v10:
time: 34.7 us; the launch traced here: 34.4 us
  Pallas kernels  33.8 us (97%)
  between operations  0.64 us (2%)
    pallas_call x1, Pallas kernels, local(): pl.pallas_call(functools.partial(kernel, n_gx, n_gy, len(operands)), out_...  32.2 us
    pallas_call x1, Pallas kernels, local(): pl.pallas_call(move, out_shape=(shape, shape), in_specs=[whole], out_spec...  1.56 us

profile of v10, /device:TPU:0, one launch (start us, length us, event | category | flops | bytes accessed | tf_op | source)
XLA Modules:
  0.0 34.4 jit_solution(3643756731633141294)
XLA Ops:
  0.6 32.2 %shard_map.230.both = f32[2,64,256]{2,1,0:T(8,128)} custom-call(f32[7,7,168]{2,1,0:T(8,128)} %refs_0_.1, bf16[160,128]{1,0:T(8,128)(2,1)} %constant.36.clone.refs_1_.refs_18_, f32[8,256]{1,0:T(8,128)} %constant.52.clone.refs_2_, f32[8,256]{1,0:T(8,128)} %refs_3_.1, f32[1,1,24]{2,1,0:T(1,128)} %refs_4_.1, f32[1,1,24]{2,1,0:T(1,128)} %refs_5_.1, ...), custom_call_target="tpu_custom_call" | custom-call | tf_op jit(solution)/shard_map/pallas_call | solution.py:621
  32.9 1.6 %shard_map.231 = (f32[7,7,168]{2,1,0:T(8,128)}, f32[7,7,168]{2,1,0:T(8,128)}) custom-call(f32[2,64,256]{2,1,0:T(8,128)} %shard_map.230.both), custom_call_target="tpu_custom_call" | custom-call | tf_op jit(solution)/shard_map/pallas_call | solution.py:645

commit v11 on v10

--- a/solution.py
+++ b/solution.py
@@ -547,7 +547,6 @@
     precondition(1)
     field_w[...] = gathered(2, w_local)
     v_field, av_rows = element(3)
-    halo_start(4, av_rows)
     av_local = av_rows[:OWN]
     partial = jnp.concatenate(
         [
@@ -565,6 +564,7 @@
     at_lane = lax.broadcasted_iota(jnp.int32, (8, 128), 1)
     packed = jnp.where(at_row == at_lane, jnp.sum(partial, axis=1, keepdims=True), 0.0)
     sums.start(jnp.sum(packed, axis=0, keepdims=True))
+    halo_start(4, av_rows)
     sums.middle()
     for turn in (1, 3, 4):
         halo_drain(turn)

time: 34.7 us -> 34.7 us (level)
  no operation moved by 1% of the time
where the time goes in v11:
time: 34.7 us; the launch traced here: 34.5 us
  Pallas kernels  33.8 us (97%)
  between operations  0.64 us (2%)
    pallas_call x1, Pallas kernels, local(): pl.pallas_call(functools.partial(kernel, n_gx, n_gy, len(operands)), out_...  32.3 us
    pallas_call x1, Pallas kernels, local(): pl.pallas_call(move, out_shape=(shape, shape), in_specs=[whole], out_spec...  1.56 us

profile of v11, /device:TPU:0, one launch (start us, length us, event | category | flops | bytes accessed | tf_op | source)
XLA Modules:
  0.0 34.5 jit_solution(13781610937852090250)
XLA Ops:
  0.6 32.3 %shard_map.230.both = f32[2,64,256]{2,1,0:T(8,128)} custom-call(f32[7,7,168]{2,1,0:T(8,128)} %refs_0_.1, bf16[160,128]{1,0:T(8,128)(2,1)} %constant.36.clone.refs_1_.refs_18_, f32[8,256]{1,0:T(8,128)} %constant.52.clone.refs_2_, f32[8,256]{1,0:T(8,128)} %refs_3_.1, f32[1,1,24]{2,1,0:T(1,128)} %refs_4_.1, f32[1,1,24]{2,1,0:T(1,128)} %refs_5_.1, ...), custom_call_target="tpu_custom_call" | custom-call | tf_op jit(solution)/shard_map/pallas_call | solution.py:621
  32.9 1.6 %shard_map.231 = (f32[7,7,168]{2,1,0:T(8,128)}, f32[7,7,168]{2,1,0:T(8,128)}) custom-call(f32[2,64,256]{2,1,0:T(8,128)} %shard_map.230.both), custom_call_target="tpu_custom_call" | custom-call | tf_op jit(solution)/shard_map/pallas_call | solution.py:645
